TPU v7x, 256 devices: a whole 4x4x8 slice. The times are simulated.
256 devices in a mesh: row: 16 (over y, z_hi), col: 16 (over x, z_lo, core).
Axes of the slice: x: 4, y: 4, z: 8 (z_hi: 4, z_lo: 2; z = z_hi * 2 + z_lo), core: 2. Of those that a mesh axis runs over, the one named last changes fastest.
Arguments:
- features: bfloat16 [65536, 512], P(('row', 'col')), may hold values from -8 to 8
- w_self: bfloat16 [512, 512], replicated, may hold values from -0.25 to 0.25
- w_neigh: bfloat16 [512, 512], replicated, may hold values from -0.25 to 0.25
- cotangent: bfloat16 [65536, 512], P(('row', 'col')), may hold values from -8 to 8
- tile_values: bfloat16 [12288, 256, 256], P(('row', 'col')), as said below
- tile_dst: int32 [12288], P(('row', 'col')), may hold values from 0 to 15
- tile_src: int32 [12288], P(('row', 'col')), may hold values from 0 to 15
- tile_count: int32 [256], P(('row', 'col')), may hold values from 1 to 47, as said below
Outputs:
- output: bfloat16 [65536, 512], P(('row', 'col'))
- grad_features: bfloat16 [65536, 512], P(('row', 'col'))
- grad_self: float32 [512, 512], replicated
- grad_neigh: float32 [512, 512], replicated
Inputs may be any that keep to these rules, and one draw needn't show every extreme that they name: `tile_count`: A is symmetric: a live slot at tiles (I, J) has a live slot at (J, I) with the transposed values, and each device's diagonal tile of its own node block (I = J = d) is live. Live slots come first, each (a, b) once; the busiest device has exactly 47 live slots. `tile_values`: entries are nonnegative; the diagonal of every node's own diagonal tile is 1 or more.
All inputs are finite; a program needn't handle non-finite values.
Results may differ from a plain program's by a relative error of at most 0.0085.
Values may be sent and summed in bfloat16 or wider, within the bound.
No kernel may reach another device: no remote copies, remote signals or barrier semaphores. Data moves between devices by JAX's collectives and lax.ppermute only.
A program may use at most 128 MiB of HBM per device.

v0:
```python
import functools

import jax
import jax.numpy as jnp
from jax import lax
from jax.experimental import pallas as pl
from jax.experimental.pallas import tpu as pltpu
from jax.sharding import PartitionSpec as P

MIB = 1 << 20
UNROLL = 4
BOTH = ("row", "col")
CONTRACT_ROWS = (((0,), (0,)), ((), ()))
CONTRACT_COLS = (((1,), (1,)), ((), ()))

GATHER = (
    (("z", 1, 3), ("z", 3, 1), ("y", 1, 3), ("y", 3, 1)),
    (("y", 1, 3), ("y", 3, 1), ("z", 1, 3), ("z", 3, 1)),
)
ROWS = ((0, 176), (176, 80))
REDUCE = (
    (("x", 1, 3), ("x", 3, 1), ("l", 1, 1)),
    (("l", 1, 1), ("x", 1, 3), ("x", 3, 1)),
)
ROW_SUM = (("y", 1, 3), ("y", 3, 1), ("z", 1, 3), ("z", 3, 1))
AXES = ("y", "z", "x", "l", "c")
SIZES = (4, 4, 4, 2, 2)


def exchange(value, step):
    axis, *masks = step
    pairs = []
    for i in range(256):
        at, rest = {}, i
        for name, size in zip(reversed(AXES), reversed(SIZES)):
            at[name], rest = rest % size, rest // size
        at[axis] ^= masks[at["c"]]
        j = 0
        for name, size in zip(AXES, SIZES):
            j = j * size + at[name]
        pairs.append((i, j))
    return lax.ppermute(value, BOTH, pairs)


def swap(value):
    return exchange(value, ("c", 1, 1))


def place(info, steps, bits, core=None):
    at = {name: info[k] for k, name in enumerate(AXES)}
    core = info[4] if core is None else core
    for step, bit in zip(steps, bits):
        if bit:
            axis, first, second = step
            at[axis] = lax.bitwise_xor(at[axis], first + core * (second - first))
    return at


def params(limit):
    return pltpu.CompilerParams(vmem_limit_bytes=limit * MIB)


VMEM = pl.BlockSpec(memory_space=pltpu.VMEM)
SMEM = pl.BlockSpec(memory_space=pltpu.SMEM)
ANY = pl.BlockSpec(memory_space=pl.ANY)


def chip_slots(info, steps, core=None):
    chips = []
    for s in range(8):
        at = place(info, steps, (s >> 2 & 1, s >> 1 & 1, s & 1), core)
        chips.append(at["x"] * 2 + at["l"])
    return chips


def degree_kernel(info, index, tiles, own, other, acc):
    count, core = index[96], info[4]
    acc[...] = jnp.zeros_like(acc)

    def add(s):
        values = tiles[s].astype(jnp.float32)
        acc[index[s]] += values[:, :128] + values[:, 128:]

    def several(group, carry):
        for k in range(UNROLL):
            add(group * UNROLL + k)
        return carry

    def single(s, carry):
        add(s)
        return carry

    groups = lax.div(count, UNROLL)
    lax.fori_loop(0, groups, several, 0)
    lax.fori_loop(groups * UNROLL, count, single, 0)

    def sums(block):
        total = jnp.sum(jnp.transpose(acc[block]), axis=0, keepdims=True)
        return jnp.broadcast_to(total, (8, total.shape[1]))

    for s, chip in enumerate(chip_slots(info, REDUCE[0])):
        own[s] = sums(chip * 2 + core)
    for s, chip in enumerate(chip_slots(info, REDUCE[0], 1 - core)):
        other[s] = sums(chip * 2 + 1 - core)


def partial_degree(info, index, tiles):
    edge = tiles.shape[1]
    return pl.pallas_call(
        degree_kernel,
        out_shape=[jax.ShapeDtypeStruct((8, 8, edge), jnp.float32)] * 2,
        in_specs=[SMEM, SMEM, VMEM],
        out_specs=[VMEM] * 2,
        scratch_shapes=[
            pltpu.VMEM((16, edge, 128), jnp.float32),
        ],
        compiler_params=params(16),
        name="degree",
    )(info, index, tiles)


def degree_stages(info, index, tiles):
    def begin(state):
        own, other = partial_degree(info, index, tiles)
        return own + swap(other)

    def add(total, part):
        for step, n in part:
            total = total[:n] + exchange(total[n:], step)
        return total

    parts = list(zip(REDUCE[0], (4, 2, 1)))
    return {
        1: begin,
        2: lambda total: add(total, parts[:2]),
        3: lambda total: add(total, parts[2:]),
    }


def spread_kernel(info, index0, index1, tiles0, tiles1, *refs):
    pieces, (send0, keep0, send1, keep1, x, acc, buf, sem, piece_sem) = refs[:4], refs[4:]
    core = info[4]
    slots = tiles0.shape[0]

    copies = []
    for chain, (steps, (first, rows)) in enumerate(zip(GATHER, ROWS)):
        for s in range(16):
            at = place(info, steps, (s & 1, s >> 1 & 1, s >> 2 & 1, s >> 3))
            block = at["y"] * 4 + at["z"]
            copies.append(
                pltpu.make_async_copy(
                    pieces[chain * 2 + s // 8].at[s % 8],
                    x.at[pl.ds(block * 2, 2), pl.ds(first, rows), :],
                    piece_sem.at[chain, s],
                )
            )
    for copy in copies:
        copy.start()

    def tile_copy(tiles, base, s):
        return pltpu.make_async_copy(tiles.at[s], buf.at[base + s], sem.at[base + s])

    first, second = index0[96], index1[96]

    def begin0(s, carry):
        tile_copy(tiles0, 0, s).start()
        return carry

    def begin1(s, carry):
        tile_copy(tiles1, slots, s).start()
        return carry

    lax.fori_loop(0, first, begin0, 0)
    lax.fori_loop(0, second, begin1, 0)

    def clear(block, carry):
        acc[block] = jnp.zeros(acc.shape[1:], acc.dtype)
        return carry

    lax.fori_loop(0, acc.shape[0], clear, 0)
    for copy in copies:
        copy.wait()

    def locate(t):
        rel = (t >= first).astype(jnp.int32)
        return t - rel * first, rel

    def arrive(t):
        s, rel = locate(t)
        tile_copy(tiles0, rel * slots, s).wait()

    def multiply(t):
        s, rel = locate(t)
        mine = rel == 0
        target = jnp.where(mine, index0[s], index1[s])
        source = jnp.where(mine, index0[48 + s], index1[48 + s])
        acc[target] += jnp.dot(
            buf[rel * slots + s], x[source * 2 + rel], preferred_element_type=jnp.float32
        )

    def several(group, carry):
        for k in range(UNROLL):
            arrive(group * UNROLL + k)
        for k in range(UNROLL):
            multiply(group * UNROLL + k)
        return carry

    def single(t, carry):
        arrive(t)
        multiply(t)
        return carry

    total = first + second
    groups = lax.div(total, UNROLL)
    lax.fori_loop(0, groups, several, 0)
    lax.fori_loop(groups * UNROLL, total, single, 0)
    for chain, (send, keep) in enumerate(((send0, keep0), (send1, keep1))):
        part = pl.ds(ROWS[chain][0], ROWS[chain][1])
        for s, chip in enumerate(chip_slots(info, REDUCE[chain])):
            for rel in range(2):
                block = chip * 2 + (core if rel == 0 else 1 - core)
                if s < 4:
                    keep[s, rel] = acc[block, part, :]
                else:
                    send[s - 4, rel] = acc[block, part, :].astype(jnp.bfloat16)


def spread(info, work, pieces):
    (index0, tiles0), (index1, tiles1) = work
    slots, edge, _ = tiles0.shape
    return pl.pallas_call(
        spread_kernel,
        out_shape=[
            jax.ShapeDtypeStruct((4, 2, rows, 256), dtype)
            for _, rows in ROWS
            for dtype in (jnp.bfloat16, jnp.float32)
        ],
        in_specs=[SMEM] * 3 + [ANY] * 6,
        out_specs=[VMEM] * 4,
        scratch_shapes=[
            pltpu.VMEM((32, edge, 256), jnp.bfloat16),
            pltpu.VMEM((16, edge, 256), jnp.float32),
            pltpu.VMEM((2 * slots, edge, edge), jnp.bfloat16),
            pltpu.SemaphoreType.DMA((2 * slots,)),
            pltpu.SemaphoreType.DMA((2, 16)),
        ],
        compiler_params=params(56),
        cost_estimate=pl.CostEstimate(
            flops=2 * 47 * edge * edge * 512, bytes_accessed=20 * MIB, transcendentals=0
        ),
        name="spread",
    )(info, index0, index1, tiles0, tiles1, *pieces)


def join_kernel(keep, got, send, rest):
    n = rest.shape[0]
    for s in range(2 * n):
        total = keep[s] + got[s].astype(jnp.float32)
        if s < n:
            rest[s] = total
        else:
            send[s - n] = total.astype(jnp.bfloat16)


def join(keep, got):
    shape = (keep.shape[0] // 2,) + keep.shape[1:]
    return pl.pallas_call(
        join_kernel,
        out_shape=[
            jax.ShapeDtypeStruct(shape, jnp.bfloat16),
            jax.ShapeDtypeStruct(shape, jnp.float32),
        ],
        in_specs=[VMEM] * 2,
        out_specs=[VMEM] * 2,
        compiler_params=params(16),
        name="join",
    )(keep, got)


def last_join_kernel(keep0, got0, keep1, got1, own, other):
    for chain, (keep, got) in enumerate(((keep0, got0), (keep1, got1))):
        part = pl.ds(ROWS[chain][0], ROWS[chain][1])
        own[part, :] = keep[0, 0] + got[0, 0].astype(jnp.float32)
        other[part, :] = keep[0, 1] + got[0, 1].astype(jnp.float32)


def last_join(keep0, got0, keep1, got1):
    edge = keep0.shape[2] + keep1.shape[2]
    return pl.pallas_call(
        last_join_kernel,
        out_shape=[jax.ShapeDtypeStruct((edge, 256), jnp.float32)] * 2,
        in_specs=[VMEM] * 4,
        out_specs=[VMEM] * 2,
        compiler_params=params(16),
        name="last_join",
    )(keep0, got0, keep1, got1)


def aggregate(info, work, own_half, arrived, stages, state):
    def beside(k, values, state):
        if k not in stages:
            return values, state
        return lax.optimization_barrier((values, stages[k](state)))

    pair = jnp.stack([own_half, arrived])
    have = [pair[None, :, first : first + rows] for first, rows in ROWS]
    for k in range(4):
        got = [exchange(h, steps[k]) for h, steps in zip(have, GATHER)]
        got, state = beside(k, got, state)
        if k < 3:
            have = [jnp.concatenate([h, g]) for h, g in zip(have, got)]
            have = lax.optimization_barrier(have)
    parts = spread(info, work, (have[0], got[0], have[1], got[1]))
    parts, state = beside(4, parts, state)
    send, keep = [parts[0], parts[2]], [parts[1], parts[3]]
    for k in range(2):
        arrived = [exchange(send[chain], REDUCE[chain][k]) for chain in range(2)]
        arrived = lax.optimization_barrier(arrived)
        arrived, state = beside(5 + k, arrived, state)
        for chain in range(2):
            send[chain], keep[chain] = join(keep[chain], arrived[chain])
        send, state = lax.optimization_barrier((send, state))
    arrived = [exchange(send[chain], REDUCE[chain][2]) for chain in range(2)]
    arrived, state = beside(7, arrived, state)
    own, other = last_join(keep[0], arrived[0], keep[1], arrived[1])
    return own, swap(other), state


def whole_width(core, own, got):
    first = core == 0
    return jnp.concatenate([jnp.where(first, own, got), jnp.where(first, got, own)], axis=1)


def dense_kernel(
    info, features, cotangent, w_self, w_neigh, degree, own, got, output, grad_pre, mean, mine, theirs
):
    deg = degree[:, 0:1]
    core = info[4]
    summed = whole_width(core, own[...], got[...])
    neighbor_mean = (summed / deg).astype(jnp.bfloat16)
    mean[...] = neighbor_mean
    preact = jnp.dot(features[...], w_self[...], preferred_element_type=jnp.float32) + jnp.dot(
        neighbor_mean, w_neigh[...], preferred_element_type=jnp.float32
    )
    part = jax.nn.sigmoid(preact)
    output[...] = (preact * part).astype(jnp.bfloat16)
    grad = (
        cotangent[...].astype(jnp.float32) * part * (1.0 + preact * (1.0 - part))
    ).astype(jnp.bfloat16)
    grad_pre[...] = grad
    back = (
        lax.dot_general(grad, w_neigh[...], CONTRACT_COLS, preferred_element_type=jnp.float32)
        / deg
    )
    mine[...] = jnp.where(core == 0, back[:, :256], back[:, 256:]).astype(jnp.bfloat16)
    theirs[...] = jnp.where(core == 0, back[:, 256:], back[:, :256]).astype(jnp.bfloat16)


def dense(info, features, cotangent, w_self, w_neigh, degree, own, got):
    nodes, width = features.shape
    full = jax.ShapeDtypeStruct((nodes, width), jnp.bfloat16)
    half = jax.ShapeDtypeStruct((nodes, 256), jnp.bfloat16)
    return pl.pallas_call(
        dense_kernel,
        out_shape=[full] * 3 + [half] * 2,
        in_specs=[SMEM] + [VMEM] * 7,
        out_specs=[VMEM] * 5,
        compiler_params=params(24),
        name="dense",
    )(info, features, cotangent, w_self, w_neigh, degree, own, got)


def weights_kernel(info, features, mean, grad_pre, w_self, keep, send, own):
    grad = grad_pre[...]
    grad_self = lax.dot_general(
        features[...], grad, CONTRACT_ROWS, preferred_element_type=jnp.float32
    )
    grad_neigh = lax.dot_general(
        mean[...], grad, CONTRACT_ROWS, preferred_element_type=jnp.float32
    )
    first = info[4] == 0
    keep[...] = jnp.where(first, grad_self, grad_neigh)
    send[...] = jnp.where(first, grad_neigh, grad_self)
    own[...] = lax.dot_general(
        grad, w_self[...], CONTRACT_COLS, preferred_element_type=jnp.float32
    )


def weights(info, features, mean, grad_pre, w_self):
    nodes, width = features.shape
    square = jax.ShapeDtypeStruct((width, width), jnp.float32)
    return pl.pallas_call(
        weights_kernel,
        out_shape=[square, square, jax.ShapeDtypeStruct((nodes, width), jnp.float32)],
        in_specs=[SMEM] + [VMEM] * 4,
        out_specs=[VMEM] * 3,
        compiler_params=params(24),
        name="weights",
    )(info, features, mean, grad_pre, w_self)


def weight_blocks_kernel(info, keep, got, send, rest):
    for s, chip in enumerate(chip_slots(info, REDUCE[0])):
        rows = pl.ds(pl.multiple_of(chip * 64, 64), 64)
        total = keep[rows, :] + got[rows, :]
        if s < 4:
            rest[s] = total
        else:
            send[s - 4] = total


def weight_blocks(info, keep, got):
    shape = jax.ShapeDtypeStruct((4, 64, keep.shape[1]), jnp.float32)
    return pl.pallas_call(
        weight_blocks_kernel,
        out_shape=[shape] * 2,
        in_specs=[SMEM, VMEM, VMEM],
        out_specs=[VMEM] * 2,
        compiler_params=params(16),
        name="weight_blocks",
    )(info, keep, got)


def weight_stages(info, features, w_self):
    steps = REDUCE[0]

    def local(state):
        grad_pre, mean = state
        keep, send, own_term = weights(info, features, mean, grad_pre, w_self)
        return keep, swap(send), own_term

    def first(state):
        keep, got, own_term = state
        send, rest = weight_blocks(info, keep, got)
        return rest + exchange(send, steps[0]), own_term

    def halve(step):
        def stage(state):
            total, own_term = state
            half = total.shape[0] // 2
            return total[:half] + exchange(total[half:], step), own_term

        return stage

    def row_sum(*chosen):
        def stage(state):
            total, own_term = state
            for step in chosen:
                total = total + exchange(total, step)
            return total, own_term

        return stage

    def collect(*chosen):
        def stage(state):
            total, own_term = state
            for step in chosen:
                total = jnp.concatenate([total, exchange(total, step)])
            return total, own_term

        return stage

    def others(total, axis):
        return [exchange(total, (axis, mask, mask)) for mask in (1, 2, 3)]

    def sum_y(state):
        total, own_term = state
        first, second, third = others(total, "y")
        return (total + first) + (second + third), own_term

    def collect_x(state):
        total, own_term = state
        return jnp.concatenate([total] + others(total, "x")), own_term

    sum_z, collect_l = row_sum(ROW_SUM[3]), collect(steps[2])
    return {
        0: local,
        1: first,
        2: halve(steps[1]),
        3: halve(steps[2]),
        4: sum_y,
        5: row_sum(ROW_SUM[2]),
        6: lambda state: collect_l(sum_z(state)),
        7: collect_x,
    }


def both_weights_kernel(info, mine, theirs, grad_self, grad_neigh):
    core = info[4]
    for value, owner in ((mine, core), (theirs, 1 - core)):
        for s in range(8):
            chip = lax.bitwise_xor(info[2], s // 2) * 2 + lax.bitwise_xor(info[3], s % 2)
            rows = pl.ds(pl.multiple_of(chip * 64, 64), 64)

            @pl.when(owner == 0)
            def _(value=value, s=s, rows=rows):
                grad_self[rows, :] = value[s]

            @pl.when(owner == 1)
            def _(value=value, s=s, rows=rows):
                grad_neigh[rows, :] = value[s]


def both_weights(info, total):
    width = total.shape[2]
    return pl.pallas_call(
        both_weights_kernel,
        out_shape=[jax.ShapeDtypeStruct((8 * total.shape[1], width), jnp.float32)] * 2,
        in_specs=[SMEM, VMEM, VMEM],
        out_specs=[VMEM] * 2,
        compiler_params=params(16),
        name="both_weights",
    )(info, total, swap(total))


def finish_kernel(info, own_term, own, got, out):
    out[...] = (own_term[...] + whole_width(info[4], own[...], got[...])).astype(jnp.bfloat16)


def finish(info, own_term, own, got):
    return pl.pallas_call(
        finish_kernel,
        out_shape=jax.ShapeDtypeStruct(own_term.shape, jnp.bfloat16),
        in_specs=[SMEM] + [VMEM] * 3,
        out_specs=VMEM,
        compiler_params=params(16),
        name="finish",
    )(info, own_term, own, got)


def shards(features, w_self, w_neigh, cotangent, tile_values, tile_dst, tile_src, tile_count):
    row, col = lax.axis_index("row"), lax.axis_index("col")
    core = col % 2
    info = jnp.stack([row // 4, row % 4, col // 4, col // 2 % 2, core]).astype(jnp.int32)
    index = jnp.concatenate([tile_dst, tile_src, tile_count])
    first = core == 0
    mine = jnp.where(first, features[:, :256], features[:, 256:])
    theirs = jnp.where(first, features[:, 256:], features[:, :256])
    theirs = swap(theirs)
    theirs, tiles = lax.optimization_barrier((theirs, tile_values))
    work = ((index, tile_values), (swap(index), swap(tiles)))
    own, got, degree = aggregate(
        info, work, mine, theirs, degree_stages(info, index, tile_values), None
    )
    degree = jnp.broadcast_to(degree[0, 0][:, None], (degree.shape[-1], 128))
    output, grad_pre, mean, mine, theirs = dense(
        info, features, cotangent, w_self, w_neigh, degree, own, got
    )
    own, got, (total, own_term) = aggregate(
        info, work, mine, swap(theirs), weight_stages(info, features, w_self), (grad_pre, mean)
    )
    grad_self, grad_neigh = both_weights(info, total)
    grad_features = finish(info, own_term, own, got)
    return (output, grad_features, grad_self, grad_neigh)


def solution(mesh):
    return jax.shard_map(
        shards,
        mesh=mesh,
        in_specs=(
            P(("row", "col"), None),
            P(),
            P(),
            P(("row", "col"), None),
            P(("row", "col"), None, None),
            P(("row", "col")),
            P(("row", "col")),
            P(("row", "col")),
        ),
        out_specs=(P(("row", "col"), None), P(("row", "col"), None), P(), P()),
        check_vma=False,
    )
```

profile of v0, /device:TPU:1, one launch (start us, length us, event | category | flops | bytes accessed | tf_op | source)
XLA Modules:
  0.0 234.2 jit_solution(12833905538655368473)
XLA Ops:
  1.7 3.3 %collective-permute-start.1 = (bf16[256,256]{1,0:T(8,128)(2,1)S(1)}, bf16[256,256]{1,0:T(8,128)(2,1)S(1)}, u32[]{:S(2)}, u32[]{:S(2)}) collective-permute-start(bf16[256,256]{1,0:T(8,128)(2,1)S(1)} %get-tuple-element.249), channel_id=1, source_target_pairs={{0,1},{1,0},{2,3},{3,2},{4,5},{5,4},{6,7},{7,6},{8,9},{9,8},{10,11... | collective-permute-start | bytes 393224 | tf_op jit(solution)/shard_map/ppermute | solution.py:42
  7.4 6.1 %collective-permute-start.3 = (bf16[1,2,176,256]{3,2,1,0:T(8,128)(2,1)S(1)}, bf16[1,2,176,256]{3,2,1,0:T(8,128)(2,1)S(1)}, u32[]{:S(2)}, u32[]{:S(2)}) collective-permute-start(bf16[1,2,176,256]{3,2,1,0:T(8,128)(2,1)S(1)} %fusion.3), channel_id=1, source_target_pairs={{0,16},{1,49},{2,18},{3,51},{4,20},{5,53},{6,22},{7,55},{8,24},{9,... | collective-permute-start | bytes 540680 | tf_op jit(solution)/shard_map/ppermute | solution.py:42
  13.5 4.3 %collective-permute-done.3 = bf16[1,2,176,256]{3,2,1,0:T(8,128)(2,1)S(1)} collective-permute-done((bf16[1,2,176,256]{3,2,1,0:T(8,128)(2,1)S(1)}, bf16[1,2,176,256]{3,2,1,0:T(8,128)(2,1)S(1)}, u32[]{:S(2)}, u32[]{:S(2)}) %collective-permute-start.3) | collective-permute-done | bytes 180256 | tf_op jit(solution)/shard_map/ppermute | solution.py:42
  24.7 3.8 %collective-permute-start.7 = (f32[8,8,256]{2,1,0:T(8,128)S(1)}, f32[8,8,256]{2,1,0:T(8,128)S(1)}, u32[]{:S(2)}, u32[]{:S(2)}) collective-permute-start(f32[8,8,256]{2,1,0:T(8,128)S(1)} %get-tuple-element.131), channel_id=1, source_target_pairs={{0,1},{1,0},{2,3},{3,2},{4,5},{5,4},{6,7},{7,6},{8,9},{9,8},{10,11... | collective-permute-start | bytes 196616 | tf_op jit(solution)/shard_map/ppermute | solution.py:42
  29.7 2.9 %collective-permute-start.10 = (f32[4,8,256]{2,1,0:T(8,128)S(1)}, f32[4,8,256]{2,1,0:T(8,128)S(1)}, u32[]{:S(2)}, u32[]{:S(2)}) collective-permute-start(f32[4,8,256]{2,1,0:T(8,128)S(1)} %slice.58), channel_id=1, source_target_pairs={{0,4},{1,13},{2,6},{3,15},{4,0},{5,9},{6,2},{7,11},{8,12},{9,5},{1... | collective-permute-start | bytes 98312 | tf_op jit(solution)/shard_map/ppermute | solution.py:42
  32.6 3.0 %collective-permute-start.9 = (bf16[4,2,80,256]{3,2,1,0:T(8,128)(2,1)S(1)}, bf16[4,2,80,256]{3,2,1,0:T(8,128)(2,1)S(1)}, u32[]{:S(2)}, u32[]{:S(2)}) collective-permute-start(bf16[4,2,80,256]{3,2,1,0:T(8,128)(2,1)S(1)} %pad_maximum_fusion.9), channel_id=1, source_target_pairs={{0,16},{1,49},{2,18},{3,51},{4,20},{5,53},{6,22},{7,55},{8,24},{9,... | collective-permute-start | bytes 983048 | tf_op jit(solution)/shard_map/ppermute | solution.py:42
  35.7 2.9 %collective-permute-done.11 = f32[2,8,256]{2,1,0:T(8,128)S(1)} collective-permute-done((f32[2,8,256]{2,1,0:T(8,128)S(1)}, f32[2,8,256]{2,1,0:T(8,128)S(1)}, u32[]{:S(2)}, u32[]{:S(2)}) %collective-permute-start.11) | collective-permute-done | bytes 16416 | tf_op jit(solution)/shard_map/ppermute | solution.py:42
  38.6 5.5 %collective-permute-done.9 = bf16[4,2,80,256]{3,2,1,0:T(8,128)(2,1)S(1)} collective-permute-done((bf16[4,2,80,256]{3,2,1,0:T(8,128)(2,1)S(1)}, bf16[4,2,80,256]{3,2,1,0:T(8,128)(2,1)S(1)}, u32[]{:S(2)}, u32[]{:S(2)}) %collective-permute-start.9) | collective-permute-done | bytes 327712 | tf_op jit(solution)/shard_map/ppermute | solution.py:42
  46.1 5.2 %collective-permute-start = (s32[97]{0:T(128)S(1)}, s32[97]{0:T(128)S(1)}, u32[]{:S(2)}, u32[]{:S(2)}) collective-permute-start(s32[97]{0:T(128)S(1)} %pad_add_fusion.index.index0), channel_id=1, source_target_pairs={{0,1},{1,0},{2,3},{3,2},{4,5},{5,4},{6,7},{7,6},{8,9},{9,8},{10,11... | collective-permute-start | bytes 1172 | tf_op jit(solution)/shard_map/ppermute | solution.py:42
  51.4 3.5 %collective-permute-done.14 = f32[1,8,256]{2,1,0:T(8,128)S(1)} collective-permute-done((f32[1,8,256]{2,1,0:T(8,128)S(1)}, f32[1,8,256]{2,1,0:T(8,128)S(1)}, u32[]{:S(2)}, u32[]{:S(2)}) %collective-permute-start.14) | collective-permute-done | bytes 8224 | tf_op jit(solution)/shard_map/ppermute | solution.py:42
  54.8 7.9 %collective-permute-done.13.refs_3_ = bf16[8,2,80,256]{3,2,1,0:T(8,128)(2,1)S(1)} collective-permute-done((bf16[8,2,80,256]{3,2,1,0:T(8,128)(2,1)S(1)}, bf16[8,2,80,256]{3,2,1,0:T(8,128)(2,1)S(1)}, u32[]{:S(2)}, u32[]{:S(2)}) %collective-permute-start.13) | collective-permute-done | bytes 655392 | tf_op jit(solution)/shard_map/ppermute | solution.py:42
  64.1 7.1 %spread.2 = (bf16[4,2,176,256]{3,2,1,0:T(8,128)(2,1)}, f32[4,2,176,256]{3,2,1,0:T(8,128)}, bf16[4,2,80,256]{3,2,1,0:T(8,128)(2,1)}, f32[4,2,80,256]{3,2,1,0:T(8,128)}) custom-call(s32[5]{0:T(128)} %copy-done.9, s32[97]{0:T(128)} %copy-done.12, s32[97]{0:T(128)} %copy-done.21, bf16[48,256,256]{2,1,0:T(8,128)(2,1)} %tiles0.3, ...), custom_call_target="tpu_custom_call" | custom-call | flops 3154116608 | bytes 20971520 | tf_op jit(solution)/shard_map/spread/pallas_call | solution.py:231
  74.9 5.4 %collective-permute-done.16.got = bf16[4,2,80,256]{3,2,1,0:T(8,128)(2,1)S(1)} collective-permute-done((bf16[4,2,80,256]{3,2,1,0:T(8,128)(2,1)}, bf16[4,2,80,256]{3,2,1,0:T(8,128)(2,1)S(1)}, u32[]{:S(2)}, u32[]{:S(2)}) %collective-permute-start.16) | collective-permute-done | bytes 327712 | tf_op jit(solution)/shard_map/ppermute | solution.py:42
  88.2 2.9 %collective-permute-done.18.got = bf16[2,2,80,256]{3,2,1,0:T(8,128)(2,1)S(1)} collective-permute-done((bf16[2,2,80,256]{3,2,1,0:T(8,128)(2,1)S(1)}, bf16[2,2,80,256]{3,2,1,0:T(8,128)(2,1)S(1)}, u32[]{:S(2)}, u32[]{:S(2)}) %collective-permute-start.18) | collective-permute-done | bytes 163872 | tf_op jit(solution)/shard_map/ppermute | solution.py:42
  92.0 3.7 %collective-permute-start.19 = (bf16[1,2,176,256]{3,2,1,0:T(8,128)(2,1)S(1)}, bf16[1,2,176,256]{3,2,1,0:T(8,128)(2,1)S(1)}, u32[]{:S(2)}, u32[]{:S(2)}) collective-permute-start(bf16[1,2,176,256]{3,2,1,0:T(8,128)(2,1)S(1)} %get-tuple-element.164), channel_id=1, source_target_pairs={{0,2},{1,3},{2,0},{3,1},{4,6},{5,7},{6,4},{7,5},{8,10},{9,11},{10,... | collective-permute-start | bytes 540680 | tf_op jit(solution)/shard_map/ppermute | solution.py:42
  95.8 3.3 %collective-permute-done.20.got1 = bf16[1,2,80,256]{3,2,1,0:T(8,128)(2,1)S(1)} collective-permute-done((bf16[1,2,80,256]{3,2,1,0:T(8,128)(2,1)S(1)}, bf16[1,2,80,256]{3,2,1,0:T(8,128)(2,1)S(1)}, u32[]{:S(2)}, u32[]{:S(2)}) %collective-permute-start.20) | collective-permute-done | bytes 81952 | tf_op jit(solution)/shard_map/ppermute | solution.py:42
  99.1 7.3 %collective-permute-start.21 = (f32[256,256]{1,0:T(8,128)S(1)}, f32[256,256]{1,0:T(8,128)S(1)}, u32[]{:S(2)}, u32[]{:S(2)}) collective-permute-start(f32[256,256]{1,0:T(8,128)S(1)} %get-tuple-element.168), channel_id=1, source_target_pairs={{0,1},{1,0},{2,3},{3,2},{4,5},{5,4},{6,7},{7,6},{8,9},{9,8},{10,11... | collective-permute-start | bytes 786440 | tf_op jit(solution)/shard_map/ppermute | solution.py:42
  113.8 3.3 %collective-permute-start.23 = (bf16[1,2,176,256]{3,2,1,0:T(8,128)(2,1)S(1)}, bf16[1,2,176,256]{3,2,1,0:T(8,128)(2,1)S(1)}, u32[]{:S(2)}, u32[]{:S(2)}) collective-permute-start(bf16[1,2,176,256]{3,2,1,0:T(8,128)(2,1)S(1)} %fusion.1), channel_id=1, source_target_pairs={{0,16},{1,49},{2,18},{3,51},{4,20},{5,53},{6,22},{7,55},{8,24},{9,... | collective-permute-start | bytes 540680 | tf_op jit(solution)/shard_map/ppermute | solution.py:42
  118.4 3.3 %collective-permute-done.24 = bf16[1,2,80,256]{3,2,1,0:T(8,128)(2,1)S(1)} collective-permute-done((bf16[1,2,80,256]{3,2,1,0:T(8,128)(2,1)S(1)}, bf16[1,2,80,256]{3,2,1,0:T(8,128)(2,1)S(1)}, u32[]{:S(2)}, u32[]{:S(2)}) %collective-permute-start.24) | collective-permute-done | bytes 81952 | tf_op jit(solution)/shard_map/ppermute | solution.py:42
  122.4 2.9 %collective-permute-start.28 = (f32[4,64,512]{2,1,0:T(8,128)S(1)}, f32[4,64,512]{2,1,0:T(8,128)S(1)}, u32[]{:S(2)}, u32[]{:S(2)}) collective-permute-start(f32[4,64,512]{2,1,0:T(8,128)S(1)} %get-tuple-element.184), channel_id=1, source_target_pairs={{0,4},{1,13},{2,6},{3,15},{4,0},{5,9},{6,2},{7,11},{8,12},{9,5},{1... | collective-permute-start | bytes 1572872 | tf_op jit(solution)/shard_map/ppermute | solution.py:42
  125.7 6.4 %collective-permute-done.28 = f32[4,64,512]{2,1,0:T(8,128)S(1)} collective-permute-done((f32[4,64,512]{2,1,0:T(8,128)S(1)}, f32[4,64,512]{2,1,0:T(8,128)S(1)}, u32[]{:S(2)}, u32[]{:S(2)}) %collective-permute-start.28) | collective-permute-done | bytes 524320 | tf_op jit(solution)/shard_map/ppermute | solution.py:42
  132.2 4.2 %collective-permute-done.26 = bf16[2,2,176,256]{3,2,1,0:T(8,128)(2,1)S(1)} collective-permute-done((bf16[2,2,176,256]{3,2,1,0:T(8,128)(2,1)S(1)}, bf16[2,2,176,256]{3,2,1,0:T(8,128)(2,1)S(1)}, u32[]{:S(2)}, u32[]{:S(2)}) %collective-permute-start.26) | collective-permute-done | bytes 360480 | tf_op jit(solution)/shard_map/ppermute | solution.py:42
  143.7 4.7 %collective-permute-done.30 = bf16[4,2,80,256]{3,2,1,0:T(8,128)(2,1)S(1)} collective-permute-done((bf16[4,2,80,256]{3,2,1,0:T(8,128)(2,1)S(1)}, bf16[4,2,80,256]{3,2,1,0:T(8,128)(2,1)S(1)}, u32[]{:S(2)}, u32[]{:S(2)}) %collective-permute-start.30) | collective-permute-done | bytes 327712 | tf_op jit(solution)/shard_map/ppermute | solution.py:42
  150.3 16.4 %collective-permute-done.34 = f32[1,64,512]{2,1,0:T(8,128)S(1)} collective-permute-done((f32[1,64,512]{2,1,0:T(8,128)S(1)}, f32[1,64,512]{2,1,0:T(8,128)S(1)}, u32[]{:S(2)}, u32[]{:S(2)}) %collective-permute-start.34) | collective-permute-done | bytes 131104 | tf_op jit(solution)/shard_map/ppermute | solution.py:42
  171.0 7.1 %spread.3 = (bf16[4,2,176,256]{3,2,1,0:T(8,128)(2,1)}, f32[4,2,176,256]{3,2,1,0:T(8,128)}, bf16[4,2,80,256]{3,2,1,0:T(8,128)(2,1)}, f32[4,2,80,256]{3,2,1,0:T(8,128)}) custom-call(s32[5]{0:T(128)} %copy-done.9, s32[97]{0:T(128)} %copy-done.12, s32[97]{0:T(128)} %copy-done.21, bf16[48,256,256]{2,1,0:T(8,128)(2,1)} %tiles0.3, ...), custom_call_target="tpu_custom_call" | custom-call | flops 3154116608 | bytes 20971520 | tf_op jit(solution)/shard_map/spread/pallas_call | solution.py:231
  178.3 3.4 %collective-permute-start.38 = (bf16[4,2,176,256]{3,2,1,0:T(8,128)(2,1)}, bf16[4,2,176,256]{3,2,1,0:T(8,128)(2,1)S(1)}, u32[]{:S(2)}, u32[]{:S(2)}) collective-permute-start(bf16[4,2,176,256]{3,2,1,0:T(8,128)(2,1)} %get-tuple-element.207), channel_id=1, source_target_pairs={{0,4},{1,13},{2,6},{3,15},{4,0},{5,9},{6,2},{7,11},{8,12},{9,5},{1... | collective-permute-start | bytes 2162696 | tf_op jit(solution)/shard_map/ppermute | solution.py:42
  185.2 6.1 %collective-permute-done.40 = f32[1,64,512]{2,1,0:T(8,128)S(1)} collective-permute-done((f32[1,64,512]{2,1,0:T(8,128)S(1)}, f32[1,64,512]{2,1,0:T(8,128)S(1)}, u32[]{:S(2)}, u32[]{:S(2)}) %collective-permute-start.40) | collective-permute-done | bytes 131104 | tf_op jit(solution)/shard_map/ppermute | solution.py:42
  192.6 3.9 %collective-permute-start.43 = (f32[1,64,512]{2,1,0:T(8,128)S(1)}, f32[1,64,512]{2,1,0:T(8,128)S(1)}, u32[]{:S(2)}, u32[]{:S(2)}) collective-permute-start(f32[1,64,512]{2,1,0:T(8,128)S(1)} %add.62), channel_id=1, source_target_pairs={{0,48},{1,17},{2,50},{3,19},{4,52},{5,21},{6,54},{7,23},{8,56},{9,... | collective-permute-start | bytes 393224 | tf_op jit(solution)/shard_map/ppermute | solution.py:42
  198.9 4.4 %collective-permute-start.44 = (f32[1,64,512]{2,1,0:T(8,128)S(1)}, f32[1,64,512]{2,1,0:T(8,128)S(1)}, u32[]{:S(2)}, u32[]{:S(2)}) collective-permute-start(f32[1,64,512]{2,1,0:T(8,128)S(1)} %add.63), channel_id=1, source_target_pairs={{0,2},{1,3},{2,0},{3,1},{4,6},{5,7},{6,4},{7,5},{8,10},{9,11},{10,... | collective-permute-start | bytes 393224 | tf_op jit(solution)/shard_map/ppermute | solution.py:42
  206.5 4.2 %collective-permute-done.42.got = bf16[2,2,80,256]{3,2,1,0:T(8,128)(2,1)S(1)} collective-permute-done((bf16[2,2,80,256]{3,2,1,0:T(8,128)(2,1)S(1)}, bf16[2,2,80,256]{3,2,1,0:T(8,128)(2,1)S(1)}, u32[]{:S(2)}, u32[]{:S(2)}) %collective-permute-start.42) | collective-permute-done | bytes 163872 | tf_op jit(solution)/shard_map/ppermute | solution.py:42
  214.3 10.8 %collective-permute-done.49 = f32[2,64,512]{2,1,0:T(8,128)S(1)} collective-permute-done((f32[2,64,512]{2,1,0:T(8,128)S(1)}, f32[2,64,512]{2,1,0:T(8,128)S(1)}, u32[]{:S(2)}, u32[]{:S(2)}) %collective-permute-start.49) | collective-permute-done | bytes 262176 | tf_op jit(solution)/shard_map/ppermute | solution.py:42
  225.2 2.9 %collective-permute-start.51 = (f32[8,64,512]{2,1,0:T(8,128)S(1)}, f32[8,64,512]{2,1,0:T(8,128)S(1)}, u32[]{:S(2)}, u32[]{:S(2)}) collective-permute-start(f32[8,64,512]{2,1,0:T(8,128)S(1)} %pad_maximum_fusion.2.mine), channel_id=1, source_target_pairs={{0,1},{1,0},{2,3},{3,2},{4,5},{5,4},{6,7},{7,6},{8,9},{9,8},{10,11... | collective-permute-start | bytes 3145736 | tf_op jit(solution)/shard_map/ppermute | solution.py:42
  (176 shorter events, 70.0 us)
Async XLA Ops:
  6.0 56.8 %collective-permute-start.2 = (bf16[48,256,256]{2,1,0:T(8,128)(2,1)}, bf16[48,256,256]{2,1,0:T(8,128)(2,1)}, u32[]{:S(2)}, u32[]{:S(2)}) collective-permute-start(bf16[48,256,256]{2,1,0:T(8,128)(2,1)} %tiles0.3), channel_id=1, source_target_pairs={{0,1},{1,0},{2,3},{3,2},{4,5},{5,4},{6,7},{7,6},{8,9},{9,8},{10,11... | collective-permute-start | bytes 18874376 | tf_op jit(solution)/shard_map/ppermute | solution.py:42
  7.4 10.5 %collective-permute-start.3 = (bf16[1,2,176,256]{3,2,1,0:T(8,128)(2,1)S(1)}, bf16[1,2,176,256]{3,2,1,0:T(8,128)(2,1)S(1)}, u32[]{:S(2)}, u32[]{:S(2)}) collective-permute-start(bf16[1,2,176,256]{3,2,1,0:T(8,128)(2,1)S(1)} %fusion.3), channel_id=1, source_target_pairs={{0,16},{1,49},{2,18},{3,51},{4,20},{5,53},{6,22},{7,55},{8,24},{9,... | collective-permute-start | bytes 540680 | tf_op jit(solution)/shard_map/ppermute | solution.py:42
  17.9 11.6 %collective-permute-start.5 = (bf16[2,2,176,256]{3,2,1,0:T(8,128)(2,1)S(1)}, bf16[2,2,176,256]{3,2,1,0:T(8,128)(2,1)S(1)}, u32[]{:S(2)}, u32[]{:S(2)}) collective-permute-start(bf16[2,2,176,256]{3,2,1,0:T(8,128)(2,1)S(1)} %pad_maximum_fusion.7), channel_id=1, source_target_pairs={{0,48},{1,17},{2,50},{3,19},{4,52},{5,21},{6,54},{7,23},{8,56},{9,... | collective-permute-start | bytes 1081352 | tf_op jit(solution)/shard_map/ppermute | solution.py:42
  20.3 9.1 %collective-permute-start.6 = (bf16[2,2,80,256]{3,2,1,0:T(8,128)(2,1)S(1)}, bf16[2,2,80,256]{3,2,1,0:T(8,128)(2,1)S(1)}, u32[]{:S(2)}, u32[]{:S(2)}) collective-permute-start(bf16[2,2,80,256]{3,2,1,0:T(8,128)(2,1)S(1)} %pad_maximum_fusion.12), channel_id=1, source_target_pairs={{0,192},{1,65},{2,194},{3,67},{4,196},{5,69},{6,198},{7,71},{8,200... | collective-permute-start | bytes 491528 | tf_op jit(solution)/shard_map/ppermute | solution.py:42
  29.6 14.6 %collective-permute-start.8 = (bf16[4,2,176,256]{3,2,1,0:T(8,128)(2,1)S(1)}, bf16[4,2,176,256]{3,2,1,0:T(8,128)(2,1)S(1)}, u32[]{:S(2)}, u32[]{:S(2)}) collective-permute-start(bf16[4,2,176,256]{3,2,1,0:T(8,128)(2,1)S(1)} %pad_maximum_fusion.3), channel_id=1, source_target_pairs={{0,64},{1,193},{2,66},{3,195},{4,68},{5,197},{6,70},{7,199},{8,72}... | collective-permute-start | bytes 2162696 | tf_op jit(solution)/shard_map/ppermute | solution.py:42
  32.6 11.5 %collective-permute-start.9 = (bf16[4,2,80,256]{3,2,1,0:T(8,128)(2,1)S(1)}, bf16[4,2,80,256]{3,2,1,0:T(8,128)(2,1)S(1)}, u32[]{:S(2)}, u32[]{:S(2)}) collective-permute-start(bf16[4,2,80,256]{3,2,1,0:T(8,128)(2,1)S(1)} %pad_maximum_fusion.9), channel_id=1, source_target_pairs={{0,16},{1,49},{2,18},{3,51},{4,20},{5,53},{6,22},{7,55},{8,24},{9,... | collective-permute-start | bytes 983048 | tf_op jit(solution)/shard_map/ppermute | solution.py:42
  44.4 18.4 %collective-permute-start.12 = (bf16[8,2,176,256]{3,2,1,0:T(8,128)(2,1)S(1)}, bf16[8,2,176,256]{3,2,1,0:T(8,128)(2,1)S(1)}, u32[]{:S(2)}, u32[]{:S(2)}) collective-permute-start(bf16[8,2,176,256]{3,2,1,0:T(8,128)(2,1)S(1)} %pad_maximum_fusion.refs_0_), channel_id=1, source_target_pairs={{0,192},{1,65},{2,194},{3,67},{4,196},{5,69},{6,198},{7,71},{8,200... | collective-permute-start | bytes 4325384 | tf_op jit(solution)/shard_map/ppermute | solution.py:42
  45.0 17.7 %collective-permute-start.13 = (bf16[8,2,80,256]{3,2,1,0:T(8,128)(2,1)S(1)}, bf16[8,2,80,256]{3,2,1,0:T(8,128)(2,1)S(1)}, u32[]{:S(2)}, u32[]{:S(2)}) collective-permute-start(bf16[8,2,80,256]{3,2,1,0:T(8,128)(2,1)S(1)} %pad_maximum_fusion.5.refs_2_), channel_id=1, source_target_pairs={{0,48},{1,17},{2,50},{3,19},{4,52},{5,21},{6,54},{7,23},{8,56},{9,... | collective-permute-start | bytes 1966088 | tf_op jit(solution)/shard_map/ppermute | solution.py:42
  45.6 9.2 %collective-permute-start.14 = (f32[1,8,256]{2,1,0:T(8,128)S(1)}, f32[1,8,256]{2,1,0:T(8,128)S(1)}, u32[]{:S(2)}, u32[]{:S(2)}) collective-permute-start(f32[1,8,256]{2,1,0:T(8,128)S(1)} %slice.62), channel_id=1, source_target_pairs={{0,2},{1,3},{2,0},{3,1},{4,6},{5,7},{6,4},{7,5},{8,10},{9,11},{10,... | collective-permute-start | bytes 24584 | tf_op jit(solution)/shard_map/ppermute | solution.py:42
  46.1 16.6 %collective-permute-start = (s32[97]{0:T(128)S(1)}, s32[97]{0:T(128)S(1)}, u32[]{:S(2)}, u32[]{:S(2)}) collective-permute-start(s32[97]{0:T(128)S(1)} %pad_add_fusion.index.index0), channel_id=1, source_target_pairs={{0,1},{1,0},{2,3},{3,2},{4,5},{5,4},{6,7},{7,6},{8,9},{9,8},{10,11... | collective-permute-start | bytes 1172 | tf_op jit(solution)/shard_map/ppermute | solution.py:42
  71.2 11.6 %collective-permute-start.15 = (bf16[4,2,176,256]{3,2,1,0:T(8,128)(2,1)}, bf16[4,2,176,256]{3,2,1,0:T(8,128)(2,1)S(1)}, u32[]{:S(2)}, u32[]{:S(2)}) collective-permute-start(bf16[4,2,176,256]{3,2,1,0:T(8,128)(2,1)} %get-tuple-element.145), channel_id=1, source_target_pairs={{0,4},{1,13},{2,6},{3,15},{4,0},{5,9},{6,2},{7,11},{8,12},{9,5},{1... | collective-permute-start | bytes 2162696 | tf_op jit(solution)/shard_map/ppermute | solution.py:42
  99.1 8.5 %collective-permute-start.21 = (f32[256,256]{1,0:T(8,128)S(1)}, f32[256,256]{1,0:T(8,128)S(1)}, u32[]{:S(2)}, u32[]{:S(2)}) collective-permute-start(f32[256,256]{1,0:T(8,128)S(1)} %get-tuple-element.168), channel_id=1, source_target_pairs={{0,1},{1,0},{2,3},{3,2},{4,5},{5,4},{6,7},{7,6},{8,9},{9,8},{10,11... | collective-permute-start | bytes 786440 | tf_op jit(solution)/shard_map/ppermute | solution.py:42
  110.8 10.9 %collective-permute-start.25 = (f32[512,512]{1,0:T(8,128)S(1)}, f32[512,512]{1,0:T(8,128)S(1)}, u32[]{:S(2)}, u32[]{:S(2)}) collective-permute-start(f32[512,512]{1,0:T(8,128)S(1)} %get-tuple-element.175), channel_id=1, source_target_pairs={{0,1},{1,0},{2,3},{3,2},{4,5},{5,4},{6,7},{7,6},{8,9},{9,8},{10,11... | collective-permute-start | bytes 3145736 | tf_op jit(solution)/shard_map/ppermute | solution.py:42
  113.8 8.0 %collective-permute-start.23 = (bf16[1,2,176,256]{3,2,1,0:T(8,128)(2,1)S(1)}, bf16[1,2,176,256]{3,2,1,0:T(8,128)(2,1)S(1)}, u32[]{:S(2)}, u32[]{:S(2)}) collective-permute-start(bf16[1,2,176,256]{3,2,1,0:T(8,128)(2,1)S(1)} %fusion.1), channel_id=1, source_target_pairs={{0,16},{1,49},{2,18},{3,51},{4,20},{5,53},{6,22},{7,55},{8,24},{9,... | collective-permute-start | bytes 540680 | tf_op jit(solution)/shard_map/ppermute | solution.py:42
  122.4 9.7 %collective-permute-start.28 = (f32[4,64,512]{2,1,0:T(8,128)S(1)}, f32[4,64,512]{2,1,0:T(8,128)S(1)}, u32[]{:S(2)}, u32[]{:S(2)}) collective-permute-start(f32[4,64,512]{2,1,0:T(8,128)S(1)} %get-tuple-element.184), channel_id=1, source_target_pairs={{0,4},{1,13},{2,6},{3,15},{4,0},{5,9},{6,2},{7,11},{8,12},{9,5},{1... | collective-permute-start | bytes 1572872 | tf_op jit(solution)/shard_map/ppermute | solution.py:42
  125.3 11.1 %collective-permute-start.26 = (bf16[2,2,176,256]{3,2,1,0:T(8,128)(2,1)S(1)}, bf16[2,2,176,256]{3,2,1,0:T(8,128)(2,1)S(1)}, u32[]{:S(2)}, u32[]{:S(2)}) collective-permute-start(bf16[2,2,176,256]{3,2,1,0:T(8,128)(2,1)S(1)} %pad_maximum_fusion.8), channel_id=1, source_target_pairs={{0,48},{1,17},{2,50},{3,19},{4,52},{5,21},{6,54},{7,23},{8,56},{9,... | collective-permute-start | bytes 1081352 | tf_op jit(solution)/shard_map/ppermute | solution.py:42
  136.6 11.8 %collective-permute-start.29 = (bf16[4,2,176,256]{3,2,1,0:T(8,128)(2,1)S(1)}, bf16[4,2,176,256]{3,2,1,0:T(8,128)(2,1)S(1)}, u32[]{:S(2)}, u32[]{:S(2)}) collective-permute-start(bf16[4,2,176,256]{3,2,1,0:T(8,128)(2,1)S(1)} %pad_maximum_fusion.4), channel_id=1, source_target_pairs={{0,64},{1,193},{2,66},{3,195},{4,68},{5,197},{6,70},{7,199},{8,72}... | collective-permute-start | bytes 2162696 | tf_op jit(solution)/shard_map/ppermute | solution.py:42
  138.1 10.2 %collective-permute-start.30 = (bf16[4,2,80,256]{3,2,1,0:T(8,128)(2,1)S(1)}, bf16[4,2,80,256]{3,2,1,0:T(8,128)(2,1)S(1)}, u32[]{:S(2)}, u32[]{:S(2)}) collective-permute-start(bf16[4,2,80,256]{3,2,1,0:T(8,128)(2,1)S(1)} %pad_maximum_fusion.10), channel_id=1, source_target_pairs={{0,16},{1,49},{2,18},{3,51},{4,20},{5,53},{6,22},{7,55},{8,24},{9,... | collective-permute-start | bytes 983048 | tf_op jit(solution)/shard_map/ppermute | solution.py:42
  148.6 18.2 %collective-permute-start.32 = (bf16[8,2,176,256]{3,2,1,0:T(8,128)(2,1)S(1)}, bf16[8,2,176,256]{3,2,1,0:T(8,128)(2,1)S(1)}, u32[]{:S(2)}, u32[]{:S(2)}) collective-permute-start(bf16[8,2,176,256]{3,2,1,0:T(8,128)(2,1)S(1)} %pad_maximum_fusion.1.refs_0_), channel_id=1, source_target_pairs={{0,192},{1,65},{2,194},{3,67},{4,196},{5,69},{6,198},{7,71},{8,200... | collective-permute-start | bytes 4325384 | tf_op jit(solution)/shard_map/ppermute | solution.py:42
  148.7 18.0 %collective-permute-start.33 = (bf16[8,2,80,256]{3,2,1,0:T(8,128)(2,1)S(1)}, bf16[8,2,80,256]{3,2,1,0:T(8,128)(2,1)S(1)}, u32[]{:S(2)}, u32[]{:S(2)}) collective-permute-start(bf16[8,2,80,256]{3,2,1,0:T(8,128)(2,1)S(1)} %pad_maximum_fusion.6.refs_2_), channel_id=1, source_target_pairs={{0,48},{1,17},{2,50},{3,19},{4,52},{5,21},{6,54},{7,23},{8,56},{9,... | collective-permute-start | bytes 1966088 | tf_op jit(solution)/shard_map/ppermute | solution.py:42
  150.2 16.5 %collective-permute-start.34 = (f32[1,64,512]{2,1,0:T(8,128)S(1)}, f32[1,64,512]{2,1,0:T(8,128)S(1)}, u32[]{:S(2)}, u32[]{:S(2)}) collective-permute-start(f32[1,64,512]{2,1,0:T(8,128)S(1)} %slice.69), channel_id=1, source_target_pairs={{0,2},{1,3},{2,0},{3,1},{4,6},{5,7},{6,4},{7,5},{8,10},{9,11},{10,... | collective-permute-start | bytes 393224 | tf_op jit(solution)/shard_map/ppermute | solution.py:42
  166.8 11.4 %collective-permute-start.37 = (f32[1,64,512]{2,1,0:T(8,128)S(1)}, f32[1,64,512]{2,1,0:T(8,128)S(1)}, u32[]{:S(2)}, u32[]{:S(2)}) collective-permute-start(f32[1,64,512]{2,1,0:T(8,128)S(1)} %slice_add_fusion.1), channel_id=1, source_target_pairs={{0,192},{1,193},{2,194},{3,195},{4,196},{5,197},{6,198},{7,199},{8... | collective-permute-start | bytes 393224 | tf_op jit(solution)/shard_map/ppermute | solution.py:42
  169.1 9.1 %collective-permute-start.36 = (f32[1,64,512]{2,1,0:T(8,128)S(1)}, f32[1,64,512]{2,1,0:T(8,128)S(1)}, u32[]{:S(2)}, u32[]{:S(2)}) collective-permute-start(f32[1,64,512]{2,1,0:T(8,128)S(1)} %slice_add_fusion.1), channel_id=1, source_target_pairs={{0,128},{1,129},{2,130},{3,131},{4,132},{5,133},{6,134},{7,135},{8... | collective-permute-start | bytes 393224 | tf_op jit(solution)/shard_map/ppermute | solution.py:42
  178.3 13.0 %collective-permute-start.38 = (bf16[4,2,176,256]{3,2,1,0:T(8,128)(2,1)}, bf16[4,2,176,256]{3,2,1,0:T(8,128)(2,1)S(1)}, u32[]{:S(2)}, u32[]{:S(2)}) collective-permute-start(bf16[4,2,176,256]{3,2,1,0:T(8,128)(2,1)} %get-tuple-element.207), channel_id=1, source_target_pairs={{0,4},{1,13},{2,6},{3,15},{4,0},{5,9},{6,2},{7,11},{8,12},{9,5},{1... | collective-permute-start | bytes 2162696 | tf_op jit(solution)/shard_map/ppermute | solution.py:42
  181.7 9.6 %collective-permute-start.39 = (bf16[4,2,80,256]{3,2,1,0:T(8,128)(2,1)}, bf16[4,2,80,256]{3,2,1,0:T(8,128)(2,1)S(1)}, u32[]{:S(2)}, u32[]{:S(2)}) collective-permute-start(bf16[4,2,80,256]{3,2,1,0:T(8,128)(2,1)} %get-tuple-element.208), channel_id=1, source_target_pairs={{0,2},{1,3},{2,0},{3,1},{4,6},{5,7},{6,4},{7,5},{8,10},{9,11},{10,... | collective-permute-start | bytes 983048 | tf_op jit(solution)/shard_map/ppermute | solution.py:42
  183.4 7.9 %collective-permute-start.40 = (f32[1,64,512]{2,1,0:T(8,128)S(1)}, f32[1,64,512]{2,1,0:T(8,128)S(1)}, u32[]{:S(2)}, u32[]{:S(2)}) collective-permute-start(f32[1,64,512]{2,1,0:T(8,128)S(1)} %add_add_fusion), channel_id=1, source_target_pairs={{0,16},{1,49},{2,18},{3,51},{4,20},{5,53},{6,22},{7,55},{8,24},{9,... | collective-permute-start | bytes 393224 | tf_op jit(solution)/shard_map/ppermute | solution.py:42
  196.5 14.2 %collective-permute-start.41 = (bf16[2,2,176,256]{3,2,1,0:T(8,128)(2,1)S(1)}, bf16[2,2,176,256]{3,2,1,0:T(8,128)(2,1)S(1)}, u32[]{:S(2)}, u32[]{:S(2)}) collective-permute-start(bf16[2,2,176,256]{3,2,1,0:T(8,128)(2,1)S(1)} %get-tuple-element.221), channel_id=1, source_target_pairs={{0,12},{1,5},{2,14},{3,7},{4,8},{5,1},{6,10},{7,3},{8,4},{9,13},{1... | collective-permute-start | bytes 1081352 | tf_op jit(solution)/shard_map/ppermute | solution.py:42
  210.8 14.3 %collective-permute-start.49 = (f32[2,64,512]{2,1,0:T(8,128)S(1)}, f32[2,64,512]{2,1,0:T(8,128)S(1)}, u32[]{:S(2)}, u32[]{:S(2)}) collective-permute-start(f32[2,64,512]{2,1,0:T(8,128)S(1)} %pad_maximum_fusion.11), channel_id=1, source_target_pairs={{0,12},{1,13},{2,14},{3,15},{4,8},{5,9},{6,10},{7,11},{8,4},{9,5},... | collective-permute-start | bytes 786440 | tf_op jit(solution)/shard_map/ppermute | solution.py:42
  211.3 13.8 %collective-permute-start.48 = (f32[2,64,512]{2,1,0:T(8,128)S(1)}, f32[2,64,512]{2,1,0:T(8,128)S(1)}, u32[]{:S(2)}, u32[]{:S(2)}) collective-permute-start(f32[2,64,512]{2,1,0:T(8,128)S(1)} %pad_maximum_fusion.11), channel_id=1, source_target_pairs={{0,8},{1,9},{2,10},{3,11},{4,12},{5,13},{6,14},{7,15},{8,0},{9,1},... | collective-permute-start | bytes 786440 | tf_op jit(solution)/shard_map/ppermute | solution.py:42
  211.3 13.8 %collective-permute-start.47 = (f32[2,64,512]{2,1,0:T(8,128)S(1)}, f32[2,64,512]{2,1,0:T(8,128)S(1)}, u32[]{:S(2)}, u32[]{:S(2)}) collective-permute-start(f32[2,64,512]{2,1,0:T(8,128)S(1)} %pad_maximum_fusion.11), channel_id=1, source_target_pairs={{0,4},{1,5},{2,6},{3,7},{4,0},{5,1},{6,2},{7,3},{8,12},{9,13},{10,... | collective-permute-start | bytes 786440 | tf_op jit(solution)/shard_map/ppermute | solution.py:42
  214.1 11.1 %collective-permute-start.45 = (bf16[1,2,176,256]{3,2,1,0:T(8,128)(2,1)S(1)}, bf16[1,2,176,256]{3,2,1,0:T(8,128)(2,1)S(1)}, u32[]{:S(2)}, u32[]{:S(2)}) collective-permute-start(bf16[1,2,176,256]{3,2,1,0:T(8,128)(2,1)S(1)} %get-tuple-element.234), channel_id=1, source_target_pairs={{0,2},{1,3},{2,0},{3,1},{4,6},{5,7},{6,4},{7,5},{8,10},{9,11},{10,... | collective-permute-start | bytes 540680 | tf_op jit(solution)/shard_map/ppermute | solution.py:42
  214.3 10.9 %collective-permute-start.46 = (bf16[1,2,80,256]{3,2,1,0:T(8,128)(2,1)S(1)}, bf16[1,2,80,256]{3,2,1,0:T(8,128)(2,1)S(1)}, u32[]{:S(2)}, u32[]{:S(2)}) collective-permute-start(bf16[1,2,80,256]{3,2,1,0:T(8,128)(2,1)S(1)} %get-tuple-element.235), channel_id=1, source_target_pairs={{0,12},{1,5},{2,14},{3,7},{4,8},{5,1},{6,10},{7,3},{8,4},{9,13},{1... | collective-permute-start | bytes 245768 | tf_op jit(solution)/shard_map/ppermute | solution.py:42
  (44 other events, 405.3 us)
where the time goes:
time: 235 us; the launch traced here: 234 us
  waiting for transfers between devices  109 us (46%)
  starting transfers between devices  88.6 us (38%)
  Pallas kernels  23.5 us (10%)
  local copies, waits for them, and re-layouts  8.45 us (4%)
    ppermute x52, waiting for transfers between devices, exchange(): return lax.ppermute(value, BOTH, pairs)  109 us
    ppermute x52, starting transfers between devices, exchange(): return lax.ppermute(value, BOTH, pairs)  88.6 us
    pallas_call x2, Pallas kernels, spread(): pl.pallas_call(spread_kernel, out_shape=[jax.ShapeDtypeStruct((4, 2, rows...  14.3 us
    unnamed x48, local copies, waits for them, and re-layouts  8.24 us
  transfers between devices with their start and end apart: 52, of which 27 were waited for; matrix products, arithmetic and copies ran while one was open for 0% of the time, Pallas kernels for 4%

commit v1 on v0

--- a/solution.py
+++ b/solution.py
@@ -315,8 +315,12 @@
     send, keep = [parts[0], parts[2]], [parts[1], parts[3]]
     for k in range(2):
         arrived = [exchange(send[chain], REDUCE[chain][k]) for chain in range(2)]
-        arrived = lax.optimization_barrier(arrived)
-        arrived, state = beside(5 + k, arrived, state)
+        if 5 + k in stages:
+            state = stages[5 + k](state)
+        if k == 1 and "after" in stages:
+            state, arrived[1] = lax.optimization_barrier((state, arrived[1]))
+            state = stages["after"](state)
+        arrived, state = lax.optimization_barrier((arrived, state))
         for chain in range(2):
             send[chain], keep[chain] = join(keep[chain], arrived[chain])
         send, state = lax.optimization_barrier((send, state))
@@ -472,7 +476,6 @@
         total, own_term = state
         return jnp.concatenate([total] + others(total, "x")), own_term
 
-    sum_z, collect_l = row_sum(ROW_SUM[3]), collect(steps[2])
     return {
         0: local,
         1: first,
@@ -480,7 +483,8 @@
         3: halve(steps[2]),
         4: sum_y,
         5: row_sum(ROW_SUM[2]),
-        6: lambda state: collect_l(sum_z(state)),
+        6: row_sum(ROW_SUM[3]),
+        "after": collect(steps[2]),
         7: collect_x,
     }
 

time: 235 us -> 233 us (level)
  waiting for transfers between devices: 109 us -> 102 us
  Pallas kernels: 23.5 us -> 26.2 us
    ppermute x52, waiting for transfers between devices: 109 us -> 102 us  [exchange(): return lax.ppermute(value, BOTH, pairs)]
    pallas_call x2, Pallas kernels: 14.3 us -> 16.8 us  [spread(): pl.pallas_call(spread_kernel, out_shape=[jax.ShapeDtypeStruct((4, 2, rows...]
  transfers between devices with their start and end apart: 52 -> 52, of which waited for: 27 -> 28; matrix products, arithmetic and copies ran while one was open for 0% -> 0% of each run, Pallas kernels for 4% -> 5%
where the time goes in v1:
time: 233 us; the launch traced here: 230 us
  waiting for transfers between devices  102 us (44%)
  starting transfers between devices  89.8 us (39%)
  Pallas kernels  26.2 us (11%)
  local copies, waits for them, and re-layouts  7.88 us (3%)
    ppermute x52, waiting for transfers between devices, exchange(): return lax.ppermute(value, BOTH, pairs)  102 us
    ppermute x52, starting transfers between devices, exchange(): return lax.ppermute(value, BOTH, pairs)  89.8 us
    pallas_call x2, Pallas kernels, spread(): pl.pallas_call(spread_kernel, out_shape=[jax.ShapeDtypeStruct((4, 2, rows...  16.8 us
    unnamed x48, local copies, waits for them, and re-layouts  7.67 us
  transfers between devices with their start and end apart: 52, of which 28 were waited for; matrix products, arithmetic and copies ran while one was open for 0% of the time, Pallas kernels for 5%

profile of v1, /device:TPU:1, one launch (start us, length us, event | category | flops | bytes accessed | tf_op | source)
XLA Modules:
  0.0 230.0 jit_solution(620829214447371381)
XLA Ops:
  1.7 3.3 %collective-permute-start.1 = (bf16[256,256]{1,0:T(8,128)(2,1)S(1)}, bf16[256,256]{1,0:T(8,128)(2,1)S(1)}, u32[]{:S(2)}, u32[]{:S(2)}) collective-permute-start(bf16[256,256]{1,0:T(8,128)(2,1)S(1)} %get-tuple-element.251), channel_id=1, source_target_pairs={{0,1},{1,0},{2,3},{3,2},{4,5},{5,4},{6,7},{7,6},{8,9},{9,8},{10,11... | collective-permute-start | bytes 393224 | tf_op jit(solution)/shard_map/ppermute | solution.py:42
  7.4 6.1 %collective-permute-start.3 = (bf16[1,2,176,256]{3,2,1,0:T(8,128)(2,1)S(1)}, bf16[1,2,176,256]{3,2,1,0:T(8,128)(2,1)S(1)}, u32[]{:S(2)}, u32[]{:S(2)}) collective-permute-start(bf16[1,2,176,256]{3,2,1,0:T(8,128)(2,1)S(1)} %fusion.3), channel_id=1, source_target_pairs={{0,16},{1,49},{2,18},{3,51},{4,20},{5,53},{6,22},{7,55},{8,24},{9,... | collective-permute-start | bytes 540680 | tf_op jit(solution)/shard_map/ppermute | solution.py:42
  13.5 4.3 %collective-permute-done.3 = bf16[1,2,176,256]{3,2,1,0:T(8,128)(2,1)S(1)} collective-permute-done((bf16[1,2,176,256]{3,2,1,0:T(8,128)(2,1)S(1)}, bf16[1,2,176,256]{3,2,1,0:T(8,128)(2,1)S(1)}, u32[]{:S(2)}, u32[]{:S(2)}) %collective-permute-start.3) | collective-permute-done | bytes 180256 | tf_op jit(solution)/shard_map/ppermute | solution.py:42
  20.5 2.8 %copy-done = bf16[48,256,256]{2,1,0:T(8,128)(2,1)S(1)} copy-done((bf16[48,256,256]{2,1,0:T(8,128)(2,1)S(1)}, bf16[48,256,256]{2,1,0:T(8,128)(2,1)}, u32[]{:S(2)}) %copy-start) | copy-done | bytes 6291480
  24.8 3.9 %collective-permute-start.7 = (f32[8,8,256]{2,1,0:T(8,128)S(1)}, f32[8,8,256]{2,1,0:T(8,128)S(1)}, u32[]{:S(2)}, u32[]{:S(2)}) collective-permute-start(f32[8,8,256]{2,1,0:T(8,128)S(1)} %get-tuple-element.132), channel_id=1, source_target_pairs={{0,1},{1,0},{2,3},{3,2},{4,5},{5,4},{6,7},{7,6},{8,9},{9,8},{10,11... | collective-permute-start | bytes 196616 | tf_op jit(solution)/shard_map/ppermute | solution.py:42
  32.5 3.2 %collective-permute-start.9 = (bf16[4,2,80,256]{3,2,1,0:T(8,128)(2,1)S(1)}, bf16[4,2,80,256]{3,2,1,0:T(8,128)(2,1)S(1)}, u32[]{:S(2)}, u32[]{:S(2)}) collective-permute-start(bf16[4,2,80,256]{3,2,1,0:T(8,128)(2,1)S(1)} %pad_maximum_fusion.9), channel_id=1, source_target_pairs={{0,16},{1,49},{2,18},{3,51},{4,20},{5,53},{6,22},{7,55},{8,24},{9,... | collective-permute-start | bytes 983048 | tf_op jit(solution)/shard_map/ppermute | solution.py:42
  35.7 2.9 %collective-permute-done.11 = f32[2,8,256]{2,1,0:T(8,128)S(1)} collective-permute-done((f32[2,8,256]{2,1,0:T(8,128)S(1)}, f32[2,8,256]{2,1,0:T(8,128)S(1)}, u32[]{:S(2)}, u32[]{:S(2)}) %collective-permute-start.11) | collective-permute-done | bytes 16416 | tf_op jit(solution)/shard_map/ppermute | solution.py:42
  38.6 3.3 %collective-permute-done.9 = bf16[4,2,80,256]{3,2,1,0:T(8,128)(2,1)S(1)} collective-permute-done((bf16[4,2,80,256]{3,2,1,0:T(8,128)(2,1)S(1)}, bf16[4,2,80,256]{3,2,1,0:T(8,128)(2,1)S(1)}, u32[]{:S(2)}, u32[]{:S(2)}) %collective-permute-start.9) | collective-permute-done | bytes 327712 | tf_op jit(solution)/shard_map/ppermute | solution.py:42
  46.1 5.2 %collective-permute-start = (s32[97]{0:T(128)S(1)}, s32[97]{0:T(128)S(1)}, u32[]{:S(2)}, u32[]{:S(2)}) collective-permute-start(s32[97]{0:T(128)S(1)} %pad_add_fusion.index.index0), channel_id=1, source_target_pairs={{0,1},{1,0},{2,3},{3,2},{4,5},{5,4},{6,7},{7,6},{8,9},{9,8},{10,11... | collective-permute-start | bytes 1172 | tf_op jit(solution)/shard_map/ppermute | solution.py:42
  51.4 3.5 %collective-permute-done.14 = f32[1,8,256]{2,1,0:T(8,128)S(1)} collective-permute-done((f32[1,8,256]{2,1,0:T(8,128)S(1)}, f32[1,8,256]{2,1,0:T(8,128)S(1)}, u32[]{:S(2)}, u32[]{:S(2)}) %collective-permute-start.14) | collective-permute-done | bytes 8224 | tf_op jit(solution)/shard_map/ppermute | solution.py:42
  54.8 6.1 %collective-permute-done.13.refs_3_ = bf16[8,2,80,256]{3,2,1,0:T(8,128)(2,1)S(1)} collective-permute-done((bf16[8,2,80,256]{3,2,1,0:T(8,128)(2,1)S(1)}, bf16[8,2,80,256]{3,2,1,0:T(8,128)(2,1)S(1)}, u32[]{:S(2)}, u32[]{:S(2)}) %collective-permute-start.13) | collective-permute-done | bytes 655392 | tf_op jit(solution)/shard_map/ppermute | solution.py:42
  62.2 8.4 %spread.2 = (bf16[4,2,176,256]{3,2,1,0:T(8,128)(2,1)}, f32[4,2,176,256]{3,2,1,0:T(8,128)}, bf16[4,2,80,256]{3,2,1,0:T(8,128)(2,1)}, f32[4,2,80,256]{3,2,1,0:T(8,128)}) custom-call(s32[5]{0:T(128)} %copy-done.9, s32[97]{0:T(128)} %copy-done.12, s32[97]{0:T(128)} %copy-done.21, bf16[48,256,256]{2,1,0:T(8,128)(2,1)} %tiles0.3, ...), custom_call_target="tpu_custom_call" | custom-call | flops 3154116608 | bytes 20971520 | tf_op jit(solution)/shard_map/spread/pallas_call | solution.py:231
  73.2 4.8 %collective-permute-done.16.got = bf16[4,2,80,256]{3,2,1,0:T(8,128)(2,1)S(1)} collective-permute-done((bf16[4,2,80,256]{3,2,1,0:T(8,128)(2,1)}, bf16[4,2,80,256]{3,2,1,0:T(8,128)(2,1)S(1)}, u32[]{:S(2)}, u32[]{:S(2)}) %collective-permute-start.16) | collective-permute-done | bytes 327712 | tf_op jit(solution)/shard_map/ppermute | solution.py:42
  78.0 4.3 %collective-permute-done.15.got = bf16[4,2,176,256]{3,2,1,0:T(8,128)(2,1)S(1)} collective-permute-done((bf16[4,2,176,256]{3,2,1,0:T(8,128)(2,1)}, bf16[4,2,176,256]{3,2,1,0:T(8,128)(2,1)S(1)}, u32[]{:S(2)}, u32[]{:S(2)}) %collective-permute-start.15) | collective-permute-done | bytes 720928 | tf_op jit(solution)/shard_map/ppermute | solution.py:42
  86.3 4.3 %collective-permute-done.18.got = bf16[2,2,80,256]{3,2,1,0:T(8,128)(2,1)S(1)} collective-permute-done((bf16[2,2,80,256]{3,2,1,0:T(8,128)(2,1)S(1)}, bf16[2,2,80,256]{3,2,1,0:T(8,128)(2,1)S(1)}, u32[]{:S(2)}, u32[]{:S(2)}) %collective-permute-start.18) | collective-permute-done | bytes 163872 | tf_op jit(solution)/shard_map/ppermute | solution.py:42
  93.6 3.9 %collective-permute-done.20.got1 = bf16[1,2,80,256]{3,2,1,0:T(8,128)(2,1)S(1)} collective-permute-done((bf16[1,2,80,256]{3,2,1,0:T(8,128)(2,1)S(1)}, bf16[1,2,80,256]{3,2,1,0:T(8,128)(2,1)S(1)}, u32[]{:S(2)}, u32[]{:S(2)}) %collective-permute-start.20) | collective-permute-done | bytes 81952 | tf_op jit(solution)/shard_map/ppermute | solution.py:42
  97.5 8.1 %collective-permute-start.21 = (f32[256,256]{1,0:T(8,128)S(1)}, f32[256,256]{1,0:T(8,128)S(1)}, u32[]{:S(2)}, u32[]{:S(2)}) collective-permute-start(f32[256,256]{1,0:T(8,128)S(1)} %get-tuple-element.171), channel_id=1, source_target_pairs={{0,1},{1,0},{2,3},{3,2},{4,5},{5,4},{6,7},{7,6},{8,9},{9,8},{10,11... | collective-permute-start | bytes 786440 | tf_op jit(solution)/shard_map/ppermute | solution.py:42
  112.9 5.3 %collective-permute-start.23 = (bf16[1,2,176,256]{3,2,1,0:T(8,128)(2,1)S(1)}, bf16[1,2,176,256]{3,2,1,0:T(8,128)(2,1)S(1)}, u32[]{:S(2)}, u32[]{:S(2)}) collective-permute-start(bf16[1,2,176,256]{3,2,1,0:T(8,128)(2,1)S(1)} %fusion.1), channel_id=1, source_target_pairs={{0,16},{1,49},{2,18},{3,51},{4,20},{5,53},{6,22},{7,55},{8,24},{9,... | collective-permute-start | bytes 540680 | tf_op jit(solution)/shard_map/ppermute | solution.py:42
  118.2 4.5 %collective-permute-done.24 = bf16[1,2,80,256]{3,2,1,0:T(8,128)(2,1)S(1)} collective-permute-done((bf16[1,2,80,256]{3,2,1,0:T(8,128)(2,1)S(1)}, bf16[1,2,80,256]{3,2,1,0:T(8,128)(2,1)S(1)}, u32[]{:S(2)}, u32[]{:S(2)}) %collective-permute-start.24) | collective-permute-done | bytes 81952 | tf_op jit(solution)/shard_map/ppermute | solution.py:42
  126.1 6.9 %collective-permute-done.28 = f32[4,64,512]{2,1,0:T(8,128)S(1)} collective-permute-done((f32[4,64,512]{2,1,0:T(8,128)S(1)}, f32[4,64,512]{2,1,0:T(8,128)S(1)}, u32[]{:S(2)}, u32[]{:S(2)}) %collective-permute-start.28) | collective-permute-done | bytes 524320 | tf_op jit(solution)/shard_map/ppermute | solution.py:42
  136.4 3.0 %collective-permute-start.30 = (bf16[4,2,80,256]{3,2,1,0:T(8,128)(2,1)S(1)}, bf16[4,2,80,256]{3,2,1,0:T(8,128)(2,1)S(1)}, u32[]{:S(2)}, u32[]{:S(2)}) collective-permute-start(bf16[4,2,80,256]{3,2,1,0:T(8,128)(2,1)S(1)} %pad_maximum_fusion.10), channel_id=1, source_target_pairs={{0,16},{1,49},{2,18},{3,51},{4,20},{5,53},{6,22},{7,55},{8,24},{9,... | collective-permute-start | bytes 983048 | tf_op jit(solution)/shard_map/ppermute | solution.py:42
  142.0 4.6 %collective-permute-done.30 = bf16[4,2,80,256]{3,2,1,0:T(8,128)(2,1)S(1)} collective-permute-done((bf16[4,2,80,256]{3,2,1,0:T(8,128)(2,1)S(1)}, bf16[4,2,80,256]{3,2,1,0:T(8,128)(2,1)S(1)}, u32[]{:S(2)}, u32[]{:S(2)}) %collective-permute-start.30) | collective-permute-done | bytes 327712 | tf_op jit(solution)/shard_map/ppermute | solution.py:42
  149.5 17.3 %collective-permute-done.34 = f32[1,64,512]{2,1,0:T(8,128)S(1)} collective-permute-done((f32[1,64,512]{2,1,0:T(8,128)S(1)}, f32[1,64,512]{2,1,0:T(8,128)S(1)}, u32[]{:S(2)}, u32[]{:S(2)}) %collective-permute-start.34) | collective-permute-done | bytes 131104 | tf_op jit(solution)/shard_map/ppermute | solution.py:42
  170.4 8.4 %spread.3 = (bf16[4,2,176,256]{3,2,1,0:T(8,128)(2,1)}, f32[4,2,176,256]{3,2,1,0:T(8,128)}, bf16[4,2,80,256]{3,2,1,0:T(8,128)(2,1)}, f32[4,2,80,256]{3,2,1,0:T(8,128)}) custom-call(s32[5]{0:T(128)} %copy-done.9, s32[97]{0:T(128)} %copy-done.12, s32[97]{0:T(128)} %copy-done.21, bf16[48,256,256]{2,1,0:T(8,128)(2,1)} %tiles0.3, ...), custom_call_target="tpu_custom_call" | custom-call | flops 3154116608 | bytes 20971520 | tf_op jit(solution)/shard_map/spread/pallas_call | solution.py:231
  179.5 3.1 %collective-permute-start.39 = (bf16[4,2,80,256]{3,2,1,0:T(8,128)(2,1)}, bf16[4,2,80,256]{3,2,1,0:T(8,128)(2,1)S(1)}, u32[]{:S(2)}, u32[]{:S(2)}) collective-permute-start(bf16[4,2,80,256]{3,2,1,0:T(8,128)(2,1)} %get-tuple-element.211), channel_id=1, source_target_pairs={{0,2},{1,3},{2,0},{3,1},{4,6},{5,7},{6,4},{7,5},{8,10},{9,11},{10,... | collective-permute-start | bytes 983048 | tf_op jit(solution)/shard_map/ppermute | solution.py:42
  184.0 6.1 %collective-permute-done.40 = f32[1,64,512]{2,1,0:T(8,128)S(1)} collective-permute-done((f32[1,64,512]{2,1,0:T(8,128)S(1)}, f32[1,64,512]{2,1,0:T(8,128)S(1)}, u32[]{:S(2)}, u32[]{:S(2)}) %collective-permute-start.40) | collective-permute-done | bytes 131104 | tf_op jit(solution)/shard_map/ppermute | solution.py:42
  193.4 4.3 %collective-permute-start.42 = (f32[1,64,512]{2,1,0:T(8,128)S(1)}, f32[1,64,512]{2,1,0:T(8,128)S(1)}, u32[]{:S(2)}, u32[]{:S(2)}) collective-permute-start(f32[1,64,512]{2,1,0:T(8,128)S(1)} %add.62), channel_id=1, source_target_pairs={{0,48},{1,17},{2,50},{3,19},{4,52},{5,21},{6,54},{7,23},{8,56},{9,... | collective-permute-start | bytes 393224 | tf_op jit(solution)/shard_map/ppermute | solution.py:42
  200.1 3.0 %collective-permute-start.44 = (f32[1,64,512]{2,1,0:T(8,128)S(1)}, f32[1,64,512]{2,1,0:T(8,128)S(1)}, u32[]{:S(2)}, u32[]{:S(2)}) collective-permute-start(f32[1,64,512]{2,1,0:T(8,128)S(1)} %add.63), channel_id=1, source_target_pairs={{0,2},{1,3},{2,0},{3,1},{4,6},{5,7},{6,4},{7,5},{8,10},{9,11},{10,... | collective-permute-start | bytes 393224 | tf_op jit(solution)/shard_map/ppermute | solution.py:42
  203.1 3.4 %collective-permute-done.44 = f32[1,64,512]{2,1,0:T(8,128)S(1)} collective-permute-done((f32[1,64,512]{2,1,0:T(8,128)S(1)}, f32[1,64,512]{2,1,0:T(8,128)S(1)}, u32[]{:S(2)}, u32[]{:S(2)}) %collective-permute-start.44) | collective-permute-done | bytes 131104 | tf_op jit(solution)/shard_map/ppermute | solution.py:42
  207.1 2.8 %collective-permute-start.48 = (f32[2,64,512]{2,1,0:T(8,128)S(1)}, f32[2,64,512]{2,1,0:T(8,128)S(1)}, u32[]{:S(2)}, u32[]{:S(2)}) collective-permute-start(f32[2,64,512]{2,1,0:T(8,128)S(1)} %pad_maximum_fusion.11), channel_id=1, source_target_pairs={{0,8},{1,9},{2,10},{3,11},{4,12},{5,13},{6,14},{7,15},{8,0},{9,1},... | collective-permute-start | bytes 786440 | tf_op jit(solution)/shard_map/ppermute | solution.py:42
  212.7 4.1 %collective-permute-done.49 = f32[2,64,512]{2,1,0:T(8,128)S(1)} collective-permute-done((f32[2,64,512]{2,1,0:T(8,128)S(1)}, f32[2,64,512]{2,1,0:T(8,128)S(1)}, u32[]{:S(2)}, u32[]{:S(2)}) %collective-permute-start.49) | collective-permute-done | bytes 262176 | tf_op jit(solution)/shard_map/ppermute | solution.py:42
  218.3 5.6 %collective-permute-start.51 = (f32[8,64,512]{2,1,0:T(8,128)S(1)}, f32[8,64,512]{2,1,0:T(8,128)S(1)}, u32[]{:S(2)}, u32[]{:S(2)}) collective-permute-start(f32[8,64,512]{2,1,0:T(8,128)S(1)} %pad_maximum_fusion.2.mine), channel_id=1, source_target_pairs={{0,1},{1,0},{2,3},{3,2},{4,5},{5,4},{6,7},{7,6},{8,9},{9,8},{10,11... | collective-permute-start | bytes 3145736 | tf_op jit(solution)/shard_map/ppermute | solution.py:42
  (176 shorter events, 67.5 us)
Async XLA Ops:
  6.0 55.0 %collective-permute-start.2 = (bf16[48,256,256]{2,1,0:T(8,128)(2,1)}, bf16[48,256,256]{2,1,0:T(8,128)(2,1)}, u32[]{:S(2)}, u32[]{:S(2)}) collective-permute-start(bf16[48,256,256]{2,1,0:T(8,128)(2,1)} %tiles0.3), channel_id=1, source_target_pairs={{0,1},{1,0},{2,3},{3,2},{4,5},{5,4},{6,7},{7,6},{8,9},{9,8},{10,11... | collective-permute-start | bytes 18874376 | tf_op jit(solution)/shard_map/ppermute | solution.py:42
  7.4 10.5 %collective-permute-start.3 = (bf16[1,2,176,256]{3,2,1,0:T(8,128)(2,1)S(1)}, bf16[1,2,176,256]{3,2,1,0:T(8,128)(2,1)S(1)}, u32[]{:S(2)}, u32[]{:S(2)}) collective-permute-start(bf16[1,2,176,256]{3,2,1,0:T(8,128)(2,1)S(1)} %fusion.3), channel_id=1, source_target_pairs={{0,16},{1,49},{2,18},{3,51},{4,20},{5,53},{6,22},{7,55},{8,24},{9,... | collective-permute-start | bytes 540680 | tf_op jit(solution)/shard_map/ppermute | solution.py:42
  17.9 11.7 %collective-permute-start.5 = (bf16[2,2,176,256]{3,2,1,0:T(8,128)(2,1)S(1)}, bf16[2,2,176,256]{3,2,1,0:T(8,128)(2,1)S(1)}, u32[]{:S(2)}, u32[]{:S(2)}) collective-permute-start(bf16[2,2,176,256]{3,2,1,0:T(8,128)(2,1)S(1)} %pad_maximum_fusion.7), channel_id=1, source_target_pairs={{0,48},{1,17},{2,50},{3,19},{4,52},{5,21},{6,54},{7,23},{8,56},{9,... | collective-permute-start | bytes 1081352 | tf_op jit(solution)/shard_map/ppermute | solution.py:42
  20.3 9.3 %collective-permute-start.6 = (bf16[2,2,80,256]{3,2,1,0:T(8,128)(2,1)S(1)}, bf16[2,2,80,256]{3,2,1,0:T(8,128)(2,1)S(1)}, u32[]{:S(2)}, u32[]{:S(2)}) collective-permute-start(bf16[2,2,80,256]{3,2,1,0:T(8,128)(2,1)S(1)} %pad_maximum_fusion.12), channel_id=1, source_target_pairs={{0,192},{1,65},{2,194},{3,67},{4,196},{5,69},{6,198},{7,71},{8,200... | collective-permute-start | bytes 491528 | tf_op jit(solution)/shard_map/ppermute | solution.py:42
  29.8 12.2 %collective-permute-start.8 = (bf16[4,2,176,256]{3,2,1,0:T(8,128)(2,1)S(1)}, bf16[4,2,176,256]{3,2,1,0:T(8,128)(2,1)S(1)}, u32[]{:S(2)}, u32[]{:S(2)}) collective-permute-start(bf16[4,2,176,256]{3,2,1,0:T(8,128)(2,1)S(1)} %pad_maximum_fusion.3), channel_id=1, source_target_pairs={{0,64},{1,193},{2,66},{3,195},{4,68},{5,197},{6,70},{7,199},{8,72}... | collective-permute-start | bytes 2162696 | tf_op jit(solution)/shard_map/ppermute | solution.py:42
  32.5 9.5 %collective-permute-start.9 = (bf16[4,2,80,256]{3,2,1,0:T(8,128)(2,1)S(1)}, bf16[4,2,80,256]{3,2,1,0:T(8,128)(2,1)S(1)}, u32[]{:S(2)}, u32[]{:S(2)}) collective-permute-start(bf16[4,2,80,256]{3,2,1,0:T(8,128)(2,1)S(1)} %pad_maximum_fusion.9), channel_id=1, source_target_pairs={{0,16},{1,49},{2,18},{3,51},{4,20},{5,53},{6,22},{7,55},{8,24},{9,... | collective-permute-start | bytes 983048 | tf_op jit(solution)/shard_map/ppermute | solution.py:42
  42.2 18.8 %collective-permute-start.12 = (bf16[8,2,176,256]{3,2,1,0:T(8,128)(2,1)S(1)}, bf16[8,2,176,256]{3,2,1,0:T(8,128)(2,1)S(1)}, u32[]{:S(2)}, u32[]{:S(2)}) collective-permute-start(bf16[8,2,176,256]{3,2,1,0:T(8,128)(2,1)S(1)} %pad_maximum_fusion.refs_0_), channel_id=1, source_target_pairs={{0,192},{1,65},{2,194},{3,67},{4,196},{5,69},{6,198},{7,71},{8,200... | collective-permute-start | bytes 4325384 | tf_op jit(solution)/shard_map/ppermute | solution.py:42
  43.1 17.8 %collective-permute-start.13 = (bf16[8,2,80,256]{3,2,1,0:T(8,128)(2,1)S(1)}, bf16[8,2,80,256]{3,2,1,0:T(8,128)(2,1)S(1)}, u32[]{:S(2)}, u32[]{:S(2)}) collective-permute-start(bf16[8,2,80,256]{3,2,1,0:T(8,128)(2,1)S(1)} %pad_maximum_fusion.5.refs_2_), channel_id=1, source_target_pairs={{0,48},{1,17},{2,50},{3,19},{4,52},{5,21},{6,54},{7,23},{8,56},{9,... | collective-permute-start | bytes 1966088 | tf_op jit(solution)/shard_map/ppermute | solution.py:42
  45.6 9.2 %collective-permute-start.14 = (f32[1,8,256]{2,1,0:T(8,128)S(1)}, f32[1,8,256]{2,1,0:T(8,128)S(1)}, u32[]{:S(2)}, u32[]{:S(2)}) collective-permute-start(f32[1,8,256]{2,1,0:T(8,128)S(1)} %slice.62), channel_id=1, source_target_pairs={{0,2},{1,3},{2,0},{3,1},{4,6},{5,7},{6,4},{7,5},{8,10},{9,11},{10,... | collective-permute-start | bytes 24584 | tf_op jit(solution)/shard_map/ppermute | solution.py:42
  46.1 14.8 %collective-permute-start = (s32[97]{0:T(128)S(1)}, s32[97]{0:T(128)S(1)}, u32[]{:S(2)}, u32[]{:S(2)}) collective-permute-start(s32[97]{0:T(128)S(1)} %pad_add_fusion.index.index0), channel_id=1, source_target_pairs={{0,1},{1,0},{2,3},{3,2},{4,5},{5,4},{6,7},{7,6},{8,9},{9,8},{10,11... | collective-permute-start | bytes 1172 | tf_op jit(solution)/shard_map/ppermute | solution.py:42
  70.7 11.6 %collective-permute-start.15 = (bf16[4,2,176,256]{3,2,1,0:T(8,128)(2,1)}, bf16[4,2,176,256]{3,2,1,0:T(8,128)(2,1)S(1)}, u32[]{:S(2)}, u32[]{:S(2)}) collective-permute-start(bf16[4,2,176,256]{3,2,1,0:T(8,128)(2,1)} %get-tuple-element.146), channel_id=1, source_target_pairs={{0,4},{1,13},{2,6},{3,15},{4,0},{5,9},{6,2},{7,11},{8,12},{9,5},{1... | collective-permute-start | bytes 2162696 | tf_op jit(solution)/shard_map/ppermute | solution.py:42
  97.5 9.2 %collective-permute-start.21 = (f32[256,256]{1,0:T(8,128)S(1)}, f32[256,256]{1,0:T(8,128)S(1)}, u32[]{:S(2)}, u32[]{:S(2)}) collective-permute-start(f32[256,256]{1,0:T(8,128)S(1)} %get-tuple-element.171), channel_id=1, source_target_pairs={{0,1},{1,0},{2,3},{3,2},{4,5},{5,4},{6,7},{7,6},{8,9},{9,8},{10,11... | collective-permute-start | bytes 786440 | tf_op jit(solution)/shard_map/ppermute | solution.py:42
  109.9 12.7 %collective-permute-start.25 = (f32[512,512]{1,0:T(8,128)S(1)}, f32[512,512]{1,0:T(8,128)S(1)}, u32[]{:S(2)}, u32[]{:S(2)}) collective-permute-start(f32[512,512]{1,0:T(8,128)S(1)} %get-tuple-element.178), channel_id=1, source_target_pairs={{0,1},{1,0},{2,3},{3,2},{4,5},{5,4},{6,7},{7,6},{8,9},{9,8},{10,11... | collective-permute-start | bytes 3145736 | tf_op jit(solution)/shard_map/ppermute | solution.py:42
  112.9 9.8 %collective-permute-start.23 = (bf16[1,2,176,256]{3,2,1,0:T(8,128)(2,1)S(1)}, bf16[1,2,176,256]{3,2,1,0:T(8,128)(2,1)S(1)}, u32[]{:S(2)}, u32[]{:S(2)}) collective-permute-start(bf16[1,2,176,256]{3,2,1,0:T(8,128)(2,1)S(1)} %fusion.1), channel_id=1, source_target_pairs={{0,16},{1,49},{2,18},{3,51},{4,20},{5,53},{6,22},{7,55},{8,24},{9,... | collective-permute-start | bytes 540680 | tf_op jit(solution)/shard_map/ppermute | solution.py:42
  123.4 9.6 %collective-permute-start.28 = (f32[4,64,512]{2,1,0:T(8,128)S(1)}, f32[4,64,512]{2,1,0:T(8,128)S(1)}, u32[]{:S(2)}, u32[]{:S(2)}) collective-permute-start(f32[4,64,512]{2,1,0:T(8,128)S(1)} %get-tuple-element.187), channel_id=1, source_target_pairs={{0,4},{1,13},{2,6},{3,15},{4,0},{5,9},{6,2},{7,11},{8,12},{9,5},{1... | collective-permute-start | bytes 1572872 | tf_op jit(solution)/shard_map/ppermute | solution.py:42
  123.9 11.2 %collective-permute-start.26 = (bf16[2,2,176,256]{3,2,1,0:T(8,128)(2,1)S(1)}, bf16[2,2,176,256]{3,2,1,0:T(8,128)(2,1)S(1)}, u32[]{:S(2)}, u32[]{:S(2)}) collective-permute-start(bf16[2,2,176,256]{3,2,1,0:T(8,128)(2,1)S(1)} %pad_maximum_fusion.8), channel_id=1, source_target_pairs={{0,48},{1,17},{2,50},{3,19},{4,52},{5,21},{6,54},{7,23},{8,56},{9,... | collective-permute-start | bytes 1081352 | tf_op jit(solution)/shard_map/ppermute | solution.py:42
  135.3 11.6 %collective-permute-start.29 = (bf16[4,2,176,256]{3,2,1,0:T(8,128)(2,1)S(1)}, bf16[4,2,176,256]{3,2,1,0:T(8,128)(2,1)S(1)}, u32[]{:S(2)}, u32[]{:S(2)}) collective-permute-start(bf16[4,2,176,256]{3,2,1,0:T(8,128)(2,1)S(1)} %pad_maximum_fusion.4), channel_id=1, source_target_pairs={{0,64},{1,193},{2,66},{3,195},{4,68},{5,197},{6,70},{7,199},{8,72}... | collective-permute-start | bytes 2162696 | tf_op jit(solution)/shard_map/ppermute | solution.py:42
  136.4 10.1 %collective-permute-start.30 = (bf16[4,2,80,256]{3,2,1,0:T(8,128)(2,1)S(1)}, bf16[4,2,80,256]{3,2,1,0:T(8,128)(2,1)S(1)}, u32[]{:S(2)}, u32[]{:S(2)}) collective-permute-start(bf16[4,2,80,256]{3,2,1,0:T(8,128)(2,1)S(1)} %pad_maximum_fusion.10), channel_id=1, source_target_pairs={{0,16},{1,49},{2,18},{3,51},{4,20},{5,53},{6,22},{7,55},{8,24},{9,... | collective-permute-start | bytes 983048 | tf_op jit(solution)/shard_map/ppermute | solution.py:42
  147.1 19.8 %collective-permute-start.32 = (bf16[8,2,176,256]{3,2,1,0:T(8,128)(2,1)S(1)}, bf16[8,2,176,256]{3,2,1,0:T(8,128)(2,1)S(1)}, u32[]{:S(2)}, u32[]{:S(2)}) collective-permute-start(bf16[8,2,176,256]{3,2,1,0:T(8,128)(2,1)S(1)} %pad_maximum_fusion.1.refs_0_), channel_id=1, source_target_pairs={{0,192},{1,65},{2,194},{3,67},{4,196},{5,69},{6,198},{7,71},{8,200... | collective-permute-start | bytes 4325384 | tf_op jit(solution)/shard_map/ppermute | solution.py:42
  147.2 19.6 %collective-permute-start.33 = (bf16[8,2,80,256]{3,2,1,0:T(8,128)(2,1)S(1)}, bf16[8,2,80,256]{3,2,1,0:T(8,128)(2,1)S(1)}, u32[]{:S(2)}, u32[]{:S(2)}) collective-permute-start(bf16[8,2,80,256]{3,2,1,0:T(8,128)(2,1)S(1)} %pad_maximum_fusion.6.refs_2_), channel_id=1, source_target_pairs={{0,48},{1,17},{2,50},{3,19},{4,52},{5,21},{6,54},{7,23},{8,56},{9,... | collective-permute-start | bytes 1966088 | tf_op jit(solution)/shard_map/ppermute | solution.py:42
  149.4 17.4 %collective-permute-start.34 = (f32[1,64,512]{2,1,0:T(8,128)S(1)}, f32[1,64,512]{2,1,0:T(8,128)S(1)}, u32[]{:S(2)}, u32[]{:S(2)}) collective-permute-start(f32[1,64,512]{2,1,0:T(8,128)S(1)} %slice.69), channel_id=1, source_target_pairs={{0,2},{1,3},{2,0},{3,1},{4,6},{5,7},{6,4},{7,5},{8,10},{9,11},{10,... | collective-permute-start | bytes 393224 | tf_op jit(solution)/shard_map/ppermute | solution.py:42
  166.8 12.0 %collective-permute-start.37 = (f32[1,64,512]{2,1,0:T(8,128)S(1)}, f32[1,64,512]{2,1,0:T(8,128)S(1)}, u32[]{:S(2)}, u32[]{:S(2)}) collective-permute-start(f32[1,64,512]{2,1,0:T(8,128)S(1)} %slice_add_fusion.1), channel_id=1, source_target_pairs={{0,192},{1,193},{2,194},{3,195},{4,196},{5,197},{6,198},{7,199},{8... | collective-permute-start | bytes 393224 | tf_op jit(solution)/shard_map/ppermute | solution.py:42
  168.7 10.2 %collective-permute-start.36 = (f32[1,64,512]{2,1,0:T(8,128)S(1)}, f32[1,64,512]{2,1,0:T(8,128)S(1)}, u32[]{:S(2)}, u32[]{:S(2)}) collective-permute-start(f32[1,64,512]{2,1,0:T(8,128)S(1)} %slice_add_fusion.1), channel_id=1, source_target_pairs={{0,128},{1,129},{2,130},{3,131},{4,132},{5,133},{6,134},{7,135},{8... | collective-permute-start | bytes 393224 | tf_op jit(solution)/shard_map/ppermute | solution.py:42
  169.8 9.1 %collective-permute-start.35 = (f32[1,64,512]{2,1,0:T(8,128)S(1)}, f32[1,64,512]{2,1,0:T(8,128)S(1)}, u32[]{:S(2)}, u32[]{:S(2)}) collective-permute-start(f32[1,64,512]{2,1,0:T(8,128)S(1)} %slice_add_fusion.1), channel_id=1, source_target_pairs={{0,64},{1,65},{2,66},{3,67},{4,68},{5,69},{6,70},{7,71},{8,72},{9,... | collective-permute-start | bytes 393224 | tf_op jit(solution)/shard_map/ppermute | solution.py:42
  178.9 11.8 %collective-permute-start.38 = (bf16[4,2,176,256]{3,2,1,0:T(8,128)(2,1)}, bf16[4,2,176,256]{3,2,1,0:T(8,128)(2,1)S(1)}, u32[]{:S(2)}, u32[]{:S(2)}) collective-permute-start(bf16[4,2,176,256]{3,2,1,0:T(8,128)(2,1)} %get-tuple-element.210), channel_id=1, source_target_pairs={{0,4},{1,13},{2,6},{3,15},{4,0},{5,9},{6,2},{7,11},{8,12},{9,5},{1... | collective-permute-start | bytes 2162696 | tf_op jit(solution)/shard_map/ppermute | solution.py:42
  179.5 10.6 %collective-permute-start.39 = (bf16[4,2,80,256]{3,2,1,0:T(8,128)(2,1)}, bf16[4,2,80,256]{3,2,1,0:T(8,128)(2,1)S(1)}, u32[]{:S(2)}, u32[]{:S(2)}) collective-permute-start(bf16[4,2,80,256]{3,2,1,0:T(8,128)(2,1)} %get-tuple-element.211), channel_id=1, source_target_pairs={{0,2},{1,3},{2,0},{3,1},{4,6},{5,7},{6,4},{7,5},{8,10},{9,11},{10,... | collective-permute-start | bytes 983048 | tf_op jit(solution)/shard_map/ppermute | solution.py:42
  192.0 8.1 %collective-permute-start.43 = (bf16[2,2,80,256]{3,2,1,0:T(8,128)(2,1)S(1)}, bf16[2,2,80,256]{3,2,1,0:T(8,128)(2,1)S(1)}, u32[]{:S(2)}, u32[]{:S(2)}) collective-permute-start(bf16[2,2,80,256]{3,2,1,0:T(8,128)(2,1)S(1)} %get-tuple-element.225), channel_id=1, source_target_pairs={{0,4},{1,13},{2,6},{3,15},{4,0},{5,9},{6,2},{7,11},{8,12},{9,5},{1... | collective-permute-start | bytes 491528 | tf_op jit(solution)/shard_map/ppermute | solution.py:42
  197.7 8.7 %collective-permute-start.41 = (bf16[2,2,176,256]{3,2,1,0:T(8,128)(2,1)S(1)}, bf16[2,2,176,256]{3,2,1,0:T(8,128)(2,1)S(1)}, u32[]{:S(2)}, u32[]{:S(2)}) collective-permute-start(bf16[2,2,176,256]{3,2,1,0:T(8,128)(2,1)S(1)} %get-tuple-element.222), channel_id=1, source_target_pairs={{0,12},{1,5},{2,14},{3,7},{4,8},{5,1},{6,10},{7,3},{8,4},{9,13},{1... | collective-permute-start | bytes 1081352 | tf_op jit(solution)/shard_map/ppermute | solution.py:42
  206.6 10.3 %collective-permute-start.49 = (f32[2,64,512]{2,1,0:T(8,128)S(1)}, f32[2,64,512]{2,1,0:T(8,128)S(1)}, u32[]{:S(2)}, u32[]{:S(2)}) collective-permute-start(f32[2,64,512]{2,1,0:T(8,128)S(1)} %pad_maximum_fusion.11), channel_id=1, source_target_pairs={{0,12},{1,13},{2,14},{3,15},{4,8},{5,9},{6,10},{7,11},{8,4},{9,5},... | collective-permute-start | bytes 786440 | tf_op jit(solution)/shard_map/ppermute | solution.py:42
  207.1 9.8 %collective-permute-start.48 = (f32[2,64,512]{2,1,0:T(8,128)S(1)}, f32[2,64,512]{2,1,0:T(8,128)S(1)}, u32[]{:S(2)}, u32[]{:S(2)}) collective-permute-start(f32[2,64,512]{2,1,0:T(8,128)S(1)} %pad_maximum_fusion.11), channel_id=1, source_target_pairs={{0,8},{1,9},{2,10},{3,11},{4,12},{5,13},{6,14},{7,15},{8,0},{9,1},... | collective-permute-start | bytes 786440 | tf_op jit(solution)/shard_map/ppermute | solution.py:42
  209.9 8.4 %collective-permute-start.45 = (bf16[1,2,176,256]{3,2,1,0:T(8,128)(2,1)S(1)}, bf16[1,2,176,256]{3,2,1,0:T(8,128)(2,1)S(1)}, u32[]{:S(2)}, u32[]{:S(2)}) collective-permute-start(bf16[1,2,176,256]{3,2,1,0:T(8,128)(2,1)S(1)} %get-tuple-element.236), channel_id=1, source_target_pairs={{0,2},{1,3},{2,0},{3,1},{4,6},{5,7},{6,4},{7,5},{8,10},{9,11},{10,... | collective-permute-start | bytes 540680 | tf_op jit(solution)/shard_map/ppermute | solution.py:42
  218.3 9.5 %collective-permute-start.51 = (f32[8,64,512]{2,1,0:T(8,128)S(1)}, f32[8,64,512]{2,1,0:T(8,128)S(1)}, u32[]{:S(2)}, u32[]{:S(2)}) collective-permute-start(f32[8,64,512]{2,1,0:T(8,128)S(1)} %pad_maximum_fusion.2.mine), channel_id=1, source_target_pairs={{0,1},{1,0},{2,3},{3,2},{4,5},{5,4},{6,7},{7,6},{8,9},{9,8},{10,11... | collective-permute-start | bytes 3145736 | tf_op jit(solution)/shard_map/ppermute | solution.py:42
  (44 other events, 402.1 us)
